TPU v7x, 32 devices: a whole 2x2x4 slice. The times are simulated.
32 devices in a mesh: ens: 4 (over y, x), oy: 2 (over core), ox: 4 (over z).
Axes of the slice: x: 2, y: 2, z: 4, core: 2. Of those that a mesh axis runs over, the one named last changes fastest.
Arguments:
- state: bfloat16 [4, 8, 512, 256], P('ens', 'oy', 'ox'), may hold values from -6 to 6
- state_cot: bfloat16 [4, 8, 512, 256], P('ens', 'oy', 'ox'), may hold values from -6 to 6
- flux_cot: bfloat16 [4, 512, 4, 128], P('ens', ('oy', 'ox')), may hold values from -6 to 6
- conv_weight: bfloat16 [9, 256, 256], replicated, may hold values from -0.125 to 0.125
- mix_weight: bfloat16 [256, 256], replicated, may hold values from -0.375 to 0.375
- flux_weight: bfloat16 [4, 256], replicated, may hold values from -3 to 3
- regrid_weights: bfloat16 [16, 128, 128], replicated, may hold values from -0.5 to 0.5
- intersection_atm: int32 [8, 4, 4], replicated, may hold values from 0 to 511, as said below
- intersection_offset: int32 [8, 4, 4], replicated, may hold values from 0 to 15
- wet_rows: int32 [2, 4], P('oy', 'ox'), may hold values from 1 to 4
Outputs:
- input_grad: bfloat16 [4, 8, 512, 256], P('ens', 'oy', 'ox')
- weight_grads: float32 [2560, 256], P(('oy', 'ox'))
- flux_grad: float32 [4, 256], replicated
Inputs may be any that keep to these rules, and one draw needn't show every extreme that they name: `intersection_atm`: atmosphere block a lies on device a // 64, numbered oy 4 + ox. The intersections of the ocean blocks of device (oy, ox), that is of latitude rows oy 4 to oy 4 + 3 and longitude block ox, lie on exactly four atmosphere devices, two with index oy and two with index (oy + 1) mod 2 along oy. At most 5 of that device's 4 x 4 intersections lie on one atmosphere device, and for every ocean device exactly 5 lie on one of them.
All inputs are finite; a program needn't handle non-finite values.
Results may differ from a plain program's by a relative error of at most 0.0085.
Values may be sent and summed in bfloat16 or wider, within the bound.
A program may use at most 64 MiB of HBM per device.

v0:
```python
import math

import jax
import jax.numpy as jnp
from jax import lax
from jax.sharding import PartitionSpec as P

CAP = 5


def with_halo(cells, sides, width):
    for axis, dim in sides:
        count = lax.axis_size(axis)
        head = lax.slice_in_dim(cells, 0, width, axis=dim)
        tail = lax.slice_in_dim(cells, cells.shape[dim] - width, cells.shape[dim], axis=dim)
        cells = jnp.concatenate(
            [
                lax.ppermute(tail, axis, [(i, (i + 1) % count) for i in range(count)]),
                cells,
                lax.ppermute(head, axis, [((i + 1) % count, i) for i in range(count)]),
            ],
            axis=dim,
        )
    return cells


def shifted(value, axis, steps):
    count = lax.axis_size(axis)
    pairs = [(source, (source + steps) % count) for source in range(count)]
    return lax.ppermute(value, axis, pairs)


def zero_ends(padded, row_index, lat_tiles):
    top_keep = jnp.where(row_index > 0, 1.0, 0.0).astype(padded.dtype)
    bottom = jnp.where(row_index < lat_tiles - 1, 1.0, 0.0).astype(padded.dtype)
    return jnp.concatenate([padded[:1] * top_keep, padded[1:-1], padded[-1:] * bottom], axis=0)


def owner_rank(owners):
    entry_count = owners.shape[-1]
    same_owner = owners[..., :, None] == owners[..., None, :]
    earlier = jnp.arange(entry_count)[None, :] < jnp.arange(entry_count)[:, None]
    return jnp.sum(jnp.logical_and(same_owner, earlier), axis=-1)


def body(
    state,
    state_cot,
    flux_cot,
    conv_weight,
    mix_weight,
    flux_weight,
    regrid_weights,
    intersection_atm,
    intersection_offset,
    wet_rows,
):
    lat_tiles = lax.axis_size("oy")
    lon_tiles = lax.axis_size("ox")
    members = lax.axis_size("ens")
    row_index = lax.axis_index("oy")
    col_index = lax.axis_index("ox")
    tile_state = state[0]
    tile_rows, block_cells, channels = tile_state.shape
    cot_flat = state_cot[0].reshape(-1, channels)
    grad_scale = 1.0 / math.sqrt(members * lat_tiles * tile_rows * lon_tiles * block_cells)
    padded = with_halo(tile_state, (("oy", 0), ("ox", 1)), 1)
    padded = zero_ends(padded, row_index, lat_tiles)
    hidden = jnp.zeros((tile_rows * block_cells, channels), jnp.float32)
    for tap_index in range(9):
        tap_row, tap_col = (tap_index // 3, tap_index % 3)
        patch_rows = padded[tap_row : tap_row + tile_rows, tap_col : tap_col + block_cells].reshape(
            -1, channels
        )
        hidden = hidden + jnp.dot(
            patch_rows, conv_weight[tap_index], preferred_element_type=jnp.float32
        )
    activation = jax.nn.silu(hidden).astype(jnp.bfloat16)
    atm_dev = flux_cot.shape[1]
    cot_blocks = flux_cot[0]
    flux_fields = cot_blocks.shape[1]
    intersections = intersection_atm.shape[2]
    entries = tile_rows * intersections
    per_dev = (
        intersection_atm.reshape(lat_tiles, tile_rows, lon_tiles, intersections)
        .transpose(0, 2, 1, 3)
        .reshape(lat_tiles, lon_tiles, entries)
    )
    per_dev_offset = (
        intersection_offset.reshape(lat_tiles, tile_rows, lon_tiles, intersections)
        .transpose(0, 2, 1, 3)
        .reshape(lat_tiles, lon_tiles, entries)
    )
    band_rows = jnp.stack([row_index, (row_index + lat_tiles - 1) % lat_tiles])
    candidate = jnp.take(per_dev, band_rows, axis=0)
    candidate_offset = jnp.take(per_dev_offset, band_rows, axis=0)
    flat_index = row_index * lon_tiles + col_index
    candidate_owner = candidate // atm_dev
    is_mine = candidate_owner == flat_index
    slot_rank = owner_rank(candidate_owner)
    local_block = jnp.where(is_mine, candidate % atm_dev, 0)
    picked_cot = cot_blocks[local_block]
    picked_maps = regrid_weights[candidate_offset]
    products = jnp.einsum(
        "qsefa,qseoa->qsefo", picked_cot, picked_maps, preferred_element_type=jnp.float32
    )
    one_hot = jnp.logical_and(
        slot_rank[..., None] == jnp.arange(CAP)[None, None, None, :], is_mine[..., None]
    ).astype(jnp.float32)
    outbound = jnp.einsum("qsec,qsefo->qscfo", one_hot, products).astype(jnp.bfloat16)
    own_entries = per_dev[row_index, col_index]
    own_owner = own_entries // atm_dev
    own_slot = owner_rank(own_owner)
    same_in, next_in = (
        lax.all_to_all(outbound[0], "ox", split_axis=0, concat_axis=0, tiled=True),
        lax.all_to_all(outbound[1], "ox", split_axis=0, concat_axis=0, tiled=True),
    )
    next_in = shifted(next_in, "oy", -1)
    arrived = jnp.concatenate([same_in, next_in], axis=0).reshape(-1, flux_fields, block_cells)
    in_next = (own_owner // lon_tiles != row_index).astype(jnp.int32)
    slot_index = (in_next * lon_tiles + own_owner % lon_tiles) * CAP + own_slot
    values = (
        arrived[slot_index]
        .astype(jnp.float32)
        .reshape(tile_rows, intersections, flux_fields, block_cells)
    )
    wet_mask = (jnp.arange(tile_rows) < wet_rows[0, 0]).astype(jnp.float32)
    flux_cells = jnp.sum(values, axis=1) * wet_mask[:, None, None]
    act_grad = lax.dot_general(
        cot_flat, mix_weight, (((1,), (1,)), ((), ())), preferred_element_type=jnp.float32
    )
    act_grad = act_grad + jnp.einsum(
        "rfb,fc->rbc", flux_cells, flux_weight.astype(jnp.float32)
    ).reshape(-1, channels)
    gate_sig = jax.nn.sigmoid(hidden)
    hidden_grad = (act_grad * gate_sig * (1.0 + hidden * (1.0 - gate_sig))).astype(jnp.bfloat16)
    padded_grad = with_halo(
        hidden_grad.reshape(tile_rows, block_cells, channels), (("oy", 0), ("ox", 1)), 1
    )
    padded_grad = zero_ends(padded_grad, row_index, lat_tiles)
    input_grad = cot_flat.astype(jnp.float32)
    tap_grads = []
    for tap_index in range(9):
        tap_row, tap_col = (tap_index // 3, tap_index % 3)
        back_rows = padded_grad[
            2 - tap_row : 2 - tap_row + tile_rows, 2 - tap_col : 2 - tap_col + block_cells
        ].reshape(-1, channels)
        input_grad = input_grad + lax.dot_general(
            back_rows,
            conv_weight[tap_index],
            (((1,), (1,)), ((), ())),
            preferred_element_type=jnp.float32,
        )
        patch_rows = padded[tap_row : tap_row + tile_rows, tap_col : tap_col + block_cells].reshape(
            -1, channels
        )
        tap_grads.append(
            lax.dot_general(
                patch_rows,
                hidden_grad,
                (((0,), (0,)), ((), ())),
                preferred_element_type=jnp.float32,
            )
        )
    tap_grads.append(
        lax.dot_general(
            activation, cot_flat, (((0,), (0,)), ((), ())), preferred_element_type=jnp.float32
        )
    )
    weight_term = jnp.concatenate(tap_grads, axis=0) * grad_scale
    flux_term = (
        jnp.einsum(
            "rfb,rbc->fc",
            flux_cells,
            activation.reshape(tile_rows, block_cells, channels).astype(jnp.float32),
        )
        * grad_scale
    )
    weight_rows = lax.psum_scatter(weight_term, ("oy", "ox"), scatter_dimension=0, tiled=True)
    weight_out = lax.psum(weight_rows, "ens")
    flux_total = lax.psum(flux_term, ("ens", "oy", "ox"))
    input_out = input_grad.reshape(1, tile_rows, block_cells, channels).astype(jnp.bfloat16)
    return (input_out, weight_out, flux_total)


def solution(mesh):
    in_specs = (
        P("ens", "oy", "ox", None),
        P("ens", "oy", "ox", None),
        P("ens", ("oy", "ox"), None, None),
        P(),
        P(),
        P(),
        P(),
        P(),
        P(),
        P("oy", "ox"),
    )
    out_specs = (P("ens", "oy", "ox", None), P(("oy", "ox"), None), P())
    return jax.shard_map(body, mesh=mesh, in_specs=in_specs, out_specs=out_specs, check_vma=False)
```

profile of v0, /device:TPU:0, one launch (start us, length us, event | category | flops | bytes accessed | tf_op | source)
XLA Modules:
  0.0 172.3 jit_solution(2728401932426398796)
XLA Ops:
  7.2 0.9 slice_bitcast_fusion.3
  8.1 0.5 collective-permute-start.1
  8.8 0.8 reshape.342
  9.8 0.8 reshape.340
  10.8 0.6 gather_fusion.4
  11.4 0.6 gather_fusion.3
  12.3 3.0 %gather_fusion.1 = bf16[128,128,128]{2,1,0:T(8,128)(2,1)} fusion(bf16[16,128,128]{2,1,0:T(8,128)(2,1)S(1)} %copy-done, s32[1024]{0:T(1024)S(1)} %get-tuple-element.48), kind=kCustom, calls=%fused_computation.3 | custom fusion | bytes 8389120 | tf_op jit(solution)/shard_map/gather | solution.py:103
  15.3 0.7 gather_fusion
  16.1 4.4 %fusion.75 = bf16[2,4,16,4,128]{4,3,2,1,0:T(4,128)(2,1)S(1)} fusion(bf16[2,4,16,4,128]{4,3,2,1,0:T(4,128)(2,1)S(1)} %bitcast.221, bf16[2,4,16,128,128]{4,3,2,1,0:T(8,128)(2,1)} %bitcast.186), kind=kOutput, calls=%fused_computation.201 | convolution fusion | flops 16777216 | bytes 4456448 | tf_op jit(solution)/shard_map/qsefa,qseoa->qsefo/dot_general | solution.py:104
  20.5 0.3 convert_reduce_fusion
  21.0 0.6 copy.27
  21.6 6.3 %all-to-all-start.1 = ((bf16[4,5,4,128]{3,2,1,0:T(4,128)(2,1)}), bf16[4,5,4,128]{3,2,1,0:T(4,128)(2,1)S(1)}, u32[]{:S(2)}, u32[]{:S(2)}) async-start(bf16[4,5,4,128]{3,2,1,0:T(4,128)(2,1)} %copy.27), calls=%async_computation.1 | async-start | bytes 40960 | tf_op jit(solution)/shard_map/all_to_all | solution.py:116
  28.4 0.6 copy.26
  29.7 3.9 %all-to-all-done.1 = bf16[4,5,4,128]{3,2,1,0:T(4,128)(2,1)S(1)} async-done(((bf16[4,5,4,128]{3,2,1,0:T(4,128)(2,1)}), bf16[4,5,4,128]{3,2,1,0:T(4,128)(2,1)S(1)}, u32[]{:S(2)}, u32[]{:S(2)}) %all-to-all-start.1) | async-done | bytes 20512 | tf_op jit(solution)/shard_map/all_to_all | solution.py:116
  33.5 3.3 %all-to-all-start = ((bf16[4,5,4,128]{3,2,1,0:T(4,128)(2,1)}), bf16[4,5,4,128]{3,2,1,0:T(4,128)(2,1)S(1)}, u32[]{:S(2)}, u32[]{:S(2)}) async-start(bf16[4,5,4,128]{3,2,1,0:T(4,128)(2,1)} %copy.26), calls=%async_computation | async-start | bytes 40960 | tf_op jit(solution)/shard_map/all_to_all | solution.py:115
  36.9 5.4 %all-to-all-done = bf16[4,5,4,128]{3,2,1,0:T(4,128)(2,1)S(1)} async-done(((bf16[4,5,4,128]{3,2,1,0:T(4,128)(2,1)}), bf16[4,5,4,128]{3,2,1,0:T(4,128)(2,1)S(1)}, u32[]{:S(2)}, u32[]{:S(2)}) %all-to-all-start) | async-done | bytes 20512 | tf_op jit(solution)/shard_map/all_to_all | solution.py:115
  42.4 0.6 gather_fusion.2
  43.1 0.7 collective-permute-start.3
  43.8 3.2 %collective-permute-start.4 = (bf16[6,1,256]{2,1,0:T(2,128)(2,1)S(1)}, bf16[6,1,256]{2,1,0:T(2,128)(2,1)S(1)}, u32[]{:S(2)}, u32[]{:S(2)}) collective-permute-start(bf16[6,1,256]{2,1,0:T(2,128)(2,1)S(1)} %get-tuple-element.20), channel_id=1, source_target_pairs={{1,0},{2,1},{3,2},{0,3},{5,4},{6,5},{7,6},{4,7},{9,8},{10,9},{11,1... | collective-permute-start | bytes 9224 | tf_op jit(solution)/shard_map/ppermute | solution.py:20
  46.9 0.3 fusion.66
  47.3 1.3 collective-permute-done.3
  50.8 0.3 multiply_convert_fusion
  51.1 0.4 copy-done.3
  51.5 0.4 fusion.6
  51.9 0.3 convolution_dynamic-update-slice_fusion.8
  52.2 0.3 convolution_dynamic-update-slice_fusion.7
  52.5 0.3 convolution_dynamic-update-slice_fusion.6
  52.7 0.3 convolution_dynamic-update-slice_fusion.5
  53.0 0.3 fusion.8
  53.3 0.3 convolution_dynamic-update-slice_fusion.4
  53.6 0.3 convolution_dynamic-update-slice_fusion.3
  53.9 0.3 convolution_dynamic-update-slice_fusion.2
  54.1 0.3 convolution_dynamic-update-slice_fusion.1
  54.4 0.3 convolution_dynamic-update-slice_fusion
  54.7 1.7 broadcast_multiply_fusion
  56.5 0.5 collective-permute-start.6
  57.3 0.5 collective-permute-done.5
  58.0 3.9 %collective-permute-start.8 = (bf16[6,1,256]{2,1,0:T(2,128)(2,1)S(1)}, bf16[6,1,256]{2,1,0:T(2,128)(2,1)S(1)}, u32[]{:S(2)}, u32[]{:S(2)}) collective-permute-start(bf16[6,1,256]{2,1,0:T(2,128)(2,1)S(1)} %get-tuple-element.16), channel_id=1, source_target_pairs={{1,0},{2,1},{3,2},{0,3},{5,4},{6,5},{7,6},{4,7},{9,8},{10,9},{11,1... | collective-permute-start | bytes 9224 | tf_op jit(solution)/shard_map/ppermute | solution.py:20
  62.1 41.4 %psum.15 = f32[4,256]{1,0:T(4,128)} all-reduce(f32[4,256]{1,0:T(4,128)S(1)} %fusion.9), channel_id=1, replica_groups=mesh['ens'=4,'oy'=2,'ox'=4] {'ens','oy','ox'}, use_global_device_ids=true, to_apply=%region_5.7 | all-reduce | flops 1024 | bytes 8192 | tf_op jit(solution)/shard_map/psum | solution.py:181
  104.3 0.3 convolution_add_fusion.6
  104.6 0.3 convolution_add_fusion.5
  104.9 0.3 convolution_add_fusion.4
  105.1 0.3 fusion.1
  105.7 12.3 %reduce-scatter.2.cloned.1.call-done = f32[320,256]{1,0:T(8,128)} async-done(((f32[2560,256]{1,0:T(8,128)}), f32[320,256]{1,0:T(8,128)}) %reduce-scatter.2.cloned.1.call-update) | async-done | bytes 327696 | tf_op jit(solution)/shard_map/reduce_scatter | solution.py:179
  118.0 0.3 convolution_add_fusion.1
  118.2 1.0 fusion.7
  119.2 44.5 %all-reduce.2.cloned.1.call-done = f32[320,256]{1,0:T(8,128)} async-done(((f32[320,256]{1,0:T(8,128)}), f32[320,256]{1,0:T(8,128)}) %all-reduce.2.cloned.1.call-update) | async-done | bytes 327696 | tf_op jit(solution)/shard_map/psum | solution.py:180
  163.7 1.7 copy.42
  (73 shorter events, 5.8 us)
Async XLA Ops:
  7.2 5.1 %copy-start = (bf16[16,128,128]{2,1,0:T(8,128)(2,1)S(1)}, bf16[16,128,128]{2,1,0:T(8,128)(2,1)}, u32[]{:S(2)}) copy-start(bf16[16,128,128]{2,1,0:T(8,128)(2,1)} %param.18) | copy-start | bytes 1572868
  8.1 34.9 %collective-permute-start.1 = (bf16[1,128,256]{2,1,0:T(8,128)(2,1)S(1)}, bf16[1,128,256]{2,1,0:T(8,128)(2,1)S(1)}, u32[]{:S(2)}, u32[]{:S(2)}) collective-permute-start(bf16[1,128,256]{2,1,0:T(8,128)(2,1)S(1)} %get-tuple-element.41), channel_id=1, source_target_pairs={{0,4},{4,0},{1,5},{5,1},{2,6},{6,2},{3,7},{7,3},{8,12},{12,8},{9,1... | collective-permute-start | bytes 196616 | tf_op jit(solution)/shard_map/ppermute | solution.py:18
  8.6 34.4 %collective-permute-start.2 = (bf16[1,128,256]{2,1,0:T(8,128)(2,1)S(1)}, bf16[1,128,256]{2,1,0:T(8,128)(2,1)S(1)}, u32[]{:S(2)}, u32[]{:S(2)}) collective-permute-start(bf16[1,128,256]{2,1,0:T(8,128)(2,1)S(1)} %get-tuple-element.42), channel_id=1, source_target_pairs={{4,0},{0,4},{5,1},{1,5},{6,2},{2,6},{7,3},{3,7},{12,8},{8,12},{13,... | collective-permute-start | bytes 196616 | tf_op jit(solution)/shard_map/ppermute | solution.py:20
  12.3 3.0 %copy-start.4 = (bf16[1,64,4,128]{3,2,1,0:T(4,128)(2,1)S(1)}, bf16[1,64,4,128]{3,2,1,0:T(4,128)(2,1)}, u32[]{:S(2)}) copy-start(bf16[1,64,4,128]{3,2,1,0:T(4,128)(2,1)} %param.14) | copy-start | bytes 196612
  15.3 12.8 %copy-start.1 = (bf16[1,4,128,256]{3,2,1,0:T(8,128)(2,1)S(1)}, bf16[1,4,128,256]{3,2,1,0:T(8,128)(2,1)}, u32[]{:S(2)}) copy-start(bf16[1,4,128,256]{3,2,1,0:T(8,128)(2,1)} %param.12) | copy-start | bytes 786436
  15.3 12.9 %copy-start.2 = (bf16[9,256,256]{2,1,0:T(8,128)(2,1)S(1)}, bf16[9,256,256]{2,1,0:T(8,128)(2,1)}, u32[]{:S(2)}) copy-start(bf16[9,256,256]{2,1,0:T(8,128)(2,1)} %param.15) | copy-start | bytes 3538948
  16.0 30.9 %copy-start.5 = (bf16[4,256]{1,0:T(4,128)(2,1)S(1)}, bf16[4,256]{1,0:T(4,128)(2,1)}, u32[]{:S(2)}) copy-start(bf16[4,256]{1,0:T(4,128)(2,1)} %param.17) | copy-start | bytes 6148
  21.6 11.9 %all-to-all-start.1 = ((bf16[4,5,4,128]{3,2,1,0:T(4,128)(2,1)}), bf16[4,5,4,128]{3,2,1,0:T(4,128)(2,1)S(1)}, u32[]{:S(2)}, u32[]{:S(2)}) async-start(bf16[4,5,4,128]{3,2,1,0:T(4,128)(2,1)} %copy.27), calls=%async_computation.1 | async-start | bytes 40960 | tf_op jit(solution)/shard_map/all_to_all | solution.py:116
  33.5 8.9 %all-to-all-start = ((bf16[4,5,4,128]{3,2,1,0:T(4,128)(2,1)}), bf16[4,5,4,128]{3,2,1,0:T(4,128)(2,1)S(1)}, u32[]{:S(2)}, u32[]{:S(2)}) async-start(bf16[4,5,4,128]{3,2,1,0:T(4,128)(2,1)} %copy.26), calls=%async_computation | async-start | bytes 40960 | tf_op jit(solution)/shard_map/all_to_all | solution.py:115
  36.8 81.2 %reduce-scatter.2.cloned.1.call-start = ((), (), s32[]{:S(2)}) async-start(), calls=%async_computation.3 | async-start | bytes 2949120 | tf_op jit(solution)/shard_map/reduce_scatter | solution.py:179
  36.8 5.5 %collective-permute-start = (bf16[4,5,4,128]{3,2,1,0:T(4,128)(2,1)S(1)}, bf16[4,5,4,128]{3,2,1,0:T(4,128)(2,1)S(1)}, u32[]{:S(2)}, u32[]{:S(2)}) collective-permute-start(bf16[4,5,4,128]{3,2,1,0:T(4,128)(2,1)S(1)} %all-to-all-done.1), channel_id=1, source_target_pairs={{0,4},{4,0},{1,5},{5,1},{2,6},{6,2},{3,7},{7,3},{8,12},{12,8},{9,1... | collective-permute-start | bytes 61448 | tf_op jit(solution)/shard_map/ppermute | solution.py:30
  43.1 5.5 %collective-permute-start.3 = (bf16[6,1,256]{2,1,0:T(2,128)(2,1)S(1)}, bf16[6,1,256]{2,1,0:T(2,128)(2,1)S(1)}, u32[]{:S(2)}, u32[]{:S(2)}) collective-permute-start(bf16[6,1,256]{2,1,0:T(2,128)(2,1)S(1)} %get-tuple-element.19), channel_id=1, source_target_pairs={{0,1},{1,2},{2,3},{3,0},{4,5},{5,6},{6,7},{7,4},{8,9},{9,10},{10,1... | collective-permute-start | bytes 9224 | tf_op jit(solution)/shard_map/ppermute | solution.py:18
  43.8 4.8 %collective-permute-start.4 = (bf16[6,1,256]{2,1,0:T(2,128)(2,1)S(1)}, bf16[6,1,256]{2,1,0:T(2,128)(2,1)S(1)}, u32[]{:S(2)}, u32[]{:S(2)}) collective-permute-start(bf16[6,1,256]{2,1,0:T(2,128)(2,1)S(1)} %get-tuple-element.20), channel_id=1, source_target_pairs={{1,0},{2,1},{3,2},{0,3},{5,4},{6,5},{7,6},{4,7},{9,8},{10,9},{11,1... | collective-permute-start | bytes 9224 | tf_op jit(solution)/shard_map/ppermute | solution.py:20
  50.6 1.0 copy-start.3
  50.6 1.0 copy-start.6
  56.4 107.3 %all-reduce.2.cloned.1.call-start = ((), (), s32[]{:S(2)}) async-start(), calls=%async_computation.4 | async-start | bytes 655360 | tf_op jit(solution)/shard_map/psum | solution.py:180
  56.5 1.3 collective-permute-start.5
  56.5 1.4 collective-permute-start.6
  58.0 45.6 %collective-permute-start.7 = (bf16[6,1,256]{2,1,0:T(2,128)(2,1)S(1)}, bf16[6,1,256]{2,1,0:T(2,128)(2,1)S(1)}, u32[]{:S(2)}, u32[]{:S(2)}) collective-permute-start(bf16[6,1,256]{2,1,0:T(2,128)(2,1)S(1)} %get-tuple-element.15), channel_id=1, source_target_pairs={{0,1},{1,2},{2,3},{3,0},{4,5},{5,6},{6,7},{7,4},{8,9},{9,10},{10,1... | collective-permute-start | bytes 9224 | tf_op jit(solution)/shard_map/ppermute | solution.py:18
  58.0 45.5 %collective-permute-start.8 = (bf16[6,1,256]{2,1,0:T(2,128)(2,1)S(1)}, bf16[6,1,256]{2,1,0:T(2,128)(2,1)S(1)}, u32[]{:S(2)}, u32[]{:S(2)}) collective-permute-start(bf16[6,1,256]{2,1,0:T(2,128)(2,1)S(1)} %get-tuple-element.16), channel_id=1, source_target_pairs={{1,0},{2,1},{3,2},{0,3},{5,4},{6,5},{7,6},{4,7},{9,8},{10,9},{11,1... | collective-permute-start | bytes 9224 | tf_op jit(solution)/shard_map/ppermute | solution.py:20
Sparse Core Ops, SparseCore 0:
  56.5 61.3 reduce-scatter.1
  120.9 42.7 all-reduce.1
where the time goes:
time: 173 us; the launch traced here: 172 us
  waiting for transfers between devices  68 us (39%)
  blocking collectives  41.4 us (24%)
  starting transfers between devices  18.7 us (11%)
  between operations  15.2 us (9%)
  matrix products  13.4 us (8%)
  local copies, waits for them, and re-layouts  12.1 us (7%)
  other arithmetic  3.51 us (2%)
    psum x1, waiting for transfers between devices, body(): weight_out = lax.psum(weight_rows, 'ens')  44.5 us
    psum x1, blocking collectives, body(): flux_total = lax.psum(flux_term, ('ens', 'oy', 'ox'))  41.4 us
    reduce_scatter x1, waiting for transfers between devices, body(): lax.psum_scatter(weight_term, ('oy', 'ox'), scatter_dimension=0, tiled=True)  12.3 us
    ppermute x4, starting transfers between devices, with_halo(): lax.ppermute(head, axis, [((i + 1) % count, i) for i in range(count)])  7.6 us
    all_to_all x1, starting transfers between devices, body(): lax.all_to_all(outbound[1], 'ox', split_axis=0, concat_axis=0, tiled=True)  6.3 us
    all_to_all x1, waiting for transfers between devices, body(): lax.all_to_all(outbound[0], 'ox', split_axis=0, concat_axis=0, tiled=True)  5.43 us
    dot_general x1, matrix products, body(): jnp.einsum('qsefa,qseoa->qsefo', picked_cot, picked_maps, preferred_eleme...  4.44 us
    all_to_all x1, waiting for transfers between devices, body(): lax.all_to_all(outbound[1], 'ox', split_axis=0, concat_axis=0, tiled=True)  3.87 us
  transfers between devices with their start and end apart: 13, of which 7 were waited for; matrix products, arithmetic and copies ran while one was open for 11% of the time, Pallas kernels for 0%

commit v1 on v0

--- a/solution.py
+++ b/solution.py
@@ -1,8 +1,11 @@
+import functools
 import math
 
 import jax
 import jax.numpy as jnp
 from jax import lax
+from jax.experimental import pallas as pl
+from jax.experimental.pallas import tpu as pltpu
 from jax.sharding import PartitionSpec as P
 
 CAP = 5
@@ -183,6 +186,426 @@
     return (input_out, weight_out, flux_total)
 
 
+F32 = jnp.float32
+BF16 = jnp.bfloat16
+MESH = pl.DeviceIdType.MESH
+EDGE = 16
+
+
+def dot(a, b, dims=((1,), (0,))):
+    return lax.dot_general(a, b, (dims, ((), ())), preferred_element_type=F32)
+
+
+def remote(src, dst, send_sem, recv_sem, target):
+    return pltpu.make_async_remote_copy(
+        src_ref=src,
+        dst_ref=dst,
+        send_sem=send_sem,
+        recv_sem=recv_sem,
+        device_id=target,
+        device_id_type=MESH,
+    )
+
+
+def start_all(copies):
+    for copy in copies:
+        copy.start()
+    return copies
+
+
+def halo_copies(src, src_at, padded, rows, cells, lat, lon, lon_tiles, sems):
+    row0, col0 = src_at
+    other = 1 - lat
+    east = lax.rem(lon + 1, lon_tiles)
+    west = lax.rem(lon + lon_tiles - 1, lon_tiles)
+    edge_row = row0 + other * (rows - 1)
+    land_row = lat * (rows + 1)
+    body_rows, dst_rows = pl.ds(row0, rows), pl.ds(1, rows)
+    head, last = pl.ds(col0, EDGE), pl.ds(col0 + cells - EDGE, EDGE)
+    left, middle, right = pl.ds(0, EDGE), pl.ds(EDGE, cells), pl.ds(EDGE + cells, EDGE)
+    plan = [
+        (src.at[pl.ds(edge_row, 1), pl.ds(col0, cells)], padded.at[pl.ds(land_row, 1), middle], other, lon),
+        (src.at[body_rows, last], padded.at[dst_rows, left], lat, east),
+        (src.at[body_rows, head], padded.at[dst_rows, right], lat, west),
+        (src.at[pl.ds(edge_row, 1), last], padded.at[pl.ds(land_row, 1), left], other, east),
+        (src.at[pl.ds(edge_row, 1), head], padded.at[pl.ds(land_row, 1), right], other, west),
+    ]
+    send, recv = sems
+    return [
+        remote(a, b, send.at[n], recv.at[n], {"oy": y, "ox": x})
+        for n, (a, b, y, x) in enumerate(plan)
+    ]
+
+
+def exchange(axis, count, me, source, target, sems, base=0):
+    send, recv = sems
+    copies = []
+    for step in range(1, count):
+        to = lax.rem(me + step, count)
+        copies.append(
+            remote(source(to), target(me), send.at[base + step - 1], recv.at[base + step - 1], {axis: to})
+        )
+    return copies
+
+
+def shift_cells(padded, wide, shifts, rows, cells):
+    for row in range(rows + 2):
+        wide[row] = padded[row].astype(F32)
+        for col in range(3):
+            shifts[col, row] = wide[row, pl.ds(EDGE - 1 + col, cells), :].astype(BF16)
+
+
+def fused_kernel(
+    sizes,
+    state,
+    cot,
+    flux_cot,
+    conv,
+    mix,
+    flux_weight,
+    regrid,
+    atm,
+    offset,
+    wet,
+    input_out,
+    weight_out,
+    flux_out,
+    padded,
+    padded_grad,
+    wide,
+    shifts,
+    turned,
+    grad_shifts,
+    entry_cell,
+    entry_map,
+    flux_send,
+    flux_recv,
+    flux_rows,
+    grads,
+    grads_half,
+    recv_lat,
+    sum_lat,
+    recv_ens,
+    sum_ens,
+    recv_lon,
+    rows_all,
+    flux_lat,
+    flux_ens,
+    flux_lon,
+    state_sems,
+    grad_sems,
+    flux_sems,
+    lat_sems,
+    ens_sems,
+    lon_sems,
+    out_sems,
+):
+    members, lat_tiles, lon_tiles, grad_scale = sizes
+    ens, lat, lon = lax.axis_index("ens"), lax.axis_index("oy"), lax.axis_index("ox")
+    rows, cells, channels = state.shape
+    fields = flux_weight.shape[0]
+    intersections = atm.shape[2]
+    maps = regrid.shape[0]
+    tiles = lat_tiles * lon_tiles
+    flat = lat * lon_tiles + lon
+    blocks = flux_cot.shape[0] // fields
+
+    barrier = pltpu.get_barrier_semaphore()
+    for step in range(1, tiles):
+        peer = lax.rem(flat + step, tiles)
+        pl.semaphore_signal(
+            barrier, inc=1, device_id={"oy": peer // lon_tiles, "ox": lax.rem(peer, lon_tiles)}, device_id_type=MESH
+        )
+    for step in range(1, members):
+        pl.semaphore_signal(
+            barrier, inc=1, device_id={"ens": lax.rem(ens + step, members)}, device_id_type=MESH
+        )
+
+    field_iota = lax.broadcasted_iota(jnp.int32, (fields, cells), 0)
+    entry = 0
+    for k in range(intersections):
+        for tile in range(tiles):
+            for row in range(rows):
+                at = ((tile // lon_tiles) * rows + row, tile % lon_tiles, k)
+                block = atm[at]
+                local = jnp.where(block // blocks == flat, lax.rem(block, blocks) * fields, -fields)
+                entry_cell[pl.ds(entry, fields), :] = field_iota + local
+                entry_map[pl.ds(entry, fields), :] = jnp.full((fields, cells), offset[at], jnp.int32)
+                entry += fields
+    which_cell = entry_cell[...]
+    which_map = entry_map[...]
+    lane = lax.broadcasted_iota(jnp.int32, which_cell.shape, 1)
+    picked = jnp.zeros(which_cell.shape, F32)
+    for part in range(blocks * fields // cells):
+        one_hot = jnp.where(which_cell == lane + part * cells, 1.0, 0.0).astype(BF16)
+        picked = picked + dot(one_hot, flux_cot[pl.ds(part * cells, cells), :])
+    products = jnp.zeros(which_cell.shape, F32)
+    for m in range(maps):
+        chosen = jnp.where(which_map == m, picked, 0.0).astype(BF16)
+        products = products + dot(chosen, regrid[m], ((1,), (1,)))
+    products = products.astype(BF16).astype(F32)
+    span = tiles * rows * fields
+    share = products[:span]
+    for k in range(1, intersections):
+        share = share + products[k * span : (k + 1) * span]
+    flux_send[...] = share.reshape(flux_send.shape)
+    flux_recv[pl.ds(flat, 1)] = flux_send[pl.ds(flat, 1)]
+
+    outside = lat * (rows + 1)
+    padded[pl.ds(outside, 1)] = jnp.zeros((1,) + padded.shape[1:], BF16)
+    padded_grad[pl.ds(outside, 1)] = jnp.zeros((1,) + padded.shape[1:], BF16)
+    padded[1 : rows + 1, EDGE : EDGE + cells] = state[...]
+    flux_rows[...] = jnp.zeros(flux_rows.shape, F32)
+    for n in range(2 * rows):
+        flux_rows[n * fields : (n + 1) * fields, :] = flux_weight[...].astype(F32)
+
+    pl.semaphore_wait(barrier, tiles - 1 + members - 1)
+    state_copies = start_all(
+        halo_copies(state, (0, 0), padded, rows, cells, lat, lon, lon_tiles, state_sems)
+    )
+    flux_copies = []
+    for step in range(1, tiles):
+        peer = lax.rem(flat + step, tiles)
+        flux_copies.append(
+            remote(
+                flux_send.at[peer],
+                flux_recv.at[flat],
+                flux_sems[0].at[step - 1],
+                flux_sems[1].at[step - 1],
+                {"oy": peer // lon_tiles, "ox": lax.rem(peer, lon_tiles)},
+            )
+        )
+    start_all(flux_copies)
+
+    cot_flat = cot[...].reshape(rows * cells, channels)
+    act_grad = dot(cot_flat, mix[...], ((1,), (1,)))
+    for copy in state_copies:
+        copy.wait_recv()
+    shift_cells(padded, wide, shifts, rows, cells)
+    hidden = jnp.zeros((rows * cells, channels), F32)
+    for tap in range(9):
+        p, q = tap // 3, tap % 3
+        hidden = hidden + dot(shifts[q, p : p + rows].reshape(rows * cells, channels), conv[tap])
+    gate = jax.nn.sigmoid(hidden)
+    activation = (hidden * gate).astype(BF16)
+    slope = gate * (1.0 + hidden * (1.0 - gate))
+    for q in range(3):
+        turned[q] = shifts[q].reshape((rows + 2) * cells, channels).T
+
+    for copy in flux_copies:
+        copy.wait_recv()
+    row_iota = lax.broadcasted_iota(jnp.int32, (rows * fields, cells), 0) // fields
+    flux = flux_recv[0]
+    for tile in range(1, tiles):
+        flux = flux + flux_recv[tile]
+    flux = jnp.where(row_iota < wet[0, 0], flux, 0.0)
+    flux_high = flux.astype(BF16).astype(F32)
+    flux_low = flux - flux_high
+    both = jnp.concatenate([flux_high, flux_low], axis=0)
+    both_iota = jnp.concatenate([row_iota, row_iota], axis=0)
+    heads = flux_rows[...].astype(BF16)
+    flux_term = jnp.zeros((2 * rows * fields, channels), F32)
+    for row in range(rows):
+        mine = jnp.where(both_iota == row, both, 0.0).astype(BF16)
+        here = slice(row * cells, (row + 1) * cells)
+        extra = dot(mine, heads, ((0,), (0,)))
+        grad = ((act_grad[here] + extra) * slope[here]).astype(BF16)
+        padded_grad[row + 1, EDGE : EDGE + cells] = grad
+        flux_term = flux_term + dot(mine, activation[here])
+    grad_copies = start_all(
+        halo_copies(padded_grad, (1, EDGE), padded_grad, rows, cells, lat, lon, lon_tiles, grad_sems)
+    )
+
+    flux_rows[...] = flux_term
+    total = flux_rows[:fields, :]
+    for n in range(1, 2 * rows):
+        total = total + flux_rows[n * fields : (n + 1) * fields, :]
+    flux_lat[pl.ds(lat, 1)] = jnp.zeros((1,) + flux_lat.shape[1:], F32)
+    flux_lat[pl.ds(lat, 1), 0:fields, :] = total[None]
+
+    hidden_grad = padded_grad[1 : rows + 1, EDGE : EDGE + cells].reshape(rows * cells, channels)
+    for tap in range(10):
+        p, q = tap // 3, tap % 3
+        if tap < 9:
+            term = dot(turned[q, :, p * cells : (p + rows) * cells], hidden_grad)
+        else:
+            term = dot(activation, cot_flat, ((0,), (0,)))
+        grads[tap * channels : (tap + 1) * channels, :] = term
+        grads_half[tap * channels : (tap + 1) * channels, :] = term.astype(BF16)
+
+    band = grads.shape[0] // lat_tiles
+    lat_copies = start_all(
+        exchange(
+            "oy",
+            lat_tiles,
+            lat,
+            lambda to: grads_half.at[pl.ds(pl.multiple_of(to * band, band), band)],
+            lambda me: recv_lat,
+            lat_sems,
+        )
+        + exchange("oy", lat_tiles, lat, lambda to: flux_lat.at[lat], lambda me: flux_lat.at[me], lat_sems, lat_tiles)
+    )
+    for copy in lat_copies:
+        copy.wait_recv()
+    own = grads[pl.ds(pl.multiple_of(lat * band, band), band), :]
+    sum_lat[...] = (own + recv_lat[...].astype(F32)).astype(BF16).reshape(sum_lat.shape)
+    total = flux_lat[0]
+    for n in range(1, lat_tiles):
+        total = total + flux_lat[n]
+    flux_ens[pl.ds(ens, 1)] = total[None]
+    ens_copies = start_all(
+        exchange("ens", members, ens, lambda to: sum_lat.at[:, to], lambda me: recv_ens.at[me], ens_sems)
+        + exchange("ens", members, ens, lambda to: flux_ens.at[ens], lambda me: flux_ens.at[me], ens_sems, members)
+    )
+    recv_ens[pl.ds(ens, 1)] = sum_lat[:, pl.ds(ens, 1)].reshape((1,) + recv_ens.shape[1:])
+
+    for copy in grad_copies:
+        copy.wait_recv()
+    shift_cells(padded_grad, wide, grad_shifts, rows, cells)
+    input_grad = cot_flat.astype(F32)
+    for tap in range(9):
+        p, q = tap // 3, tap % 3
+        back = grad_shifts[2 - q, 2 - p : 2 - p + rows].reshape(rows * cells, channels)
+        input_grad = input_grad + dot(back, conv[tap], ((1,), (1,)))
+    input_out[...] = input_grad.astype(BF16).reshape(input_out.shape)
+
+    for copy in ens_copies:
+        copy.wait_recv()
+    total = recv_ens[0].astype(F32)
+    for n in range(1, members):
+        total = total + recv_ens[n].astype(F32)
+    sum_ens[...] = total.astype(BF16)
+    total = flux_ens[0]
+    for n in range(1, members):
+        total = total + flux_ens[n]
+    flux_lon[pl.ds(lon, 1)] = total[None]
+    lon_copies = start_all(
+        exchange("ox", lon_tiles, lon, lambda to: sum_ens.at[to], lambda me: recv_lon.at[me], lon_sems)
+        + exchange("ox", lon_tiles, lon, lambda to: flux_lon.at[lon], lambda me: flux_lon.at[me], lon_sems, lon_tiles)
+    )
+    recv_lon[pl.ds(lon, 1)] = sum_ens[pl.ds(lon, 1)]
+    for copy in lon_copies:
+        copy.wait_recv()
+    total = recv_lon[0].astype(F32)
+    for n in range(1, lon_tiles):
+        total = total + recv_lon[n].astype(F32)
+    rows_all[pl.ds(ens, 1)] = (total * grad_scale).astype(BF16)[None]
+    out_copies = start_all(
+        exchange("ens", members, ens, lambda to: rows_all.at[ens], lambda me: rows_all.at[me], out_sems)
+    )
+    total = flux_lon[0]
+    for n in range(1, lon_tiles):
+        total = total + flux_lon[n]
+    flux_out[...] = total[:fields] * grad_scale
+    for copy in out_copies:
+        copy.wait_recv()
+    weight_out[...] = rows_all[...].astype(F32).reshape(weight_out.shape)
+    for copy in state_copies + flux_copies + grad_copies + lat_copies + ens_copies + lon_copies + out_copies:
+        copy.wait_send()
+
+
+def fused_body(
+    state,
+    state_cot,
+    flux_cot,
+    conv_weight,
+    mix_weight,
+    flux_weight,
+    regrid_weights,
+    intersection_atm,
+    intersection_offset,
+    wet_rows,
+):
+    members, lat_tiles, lon_tiles = (lax.axis_size(name) for name in ("ens", "oy", "ox"))
+    tile = state.shape[1:]
+    rows, cells, channels = tile
+    fields = flux_weight.shape[0]
+    tiles = lat_tiles * lon_tiles
+    grad_rows = (conv_weight.shape[0] + 1) * channels
+    band = grad_rows // lat_tiles
+    sub = band // lon_tiles // members
+    grad_scale = 1.0 / math.sqrt(members * lat_tiles * rows * lon_tiles * cells)
+    entries = tiles * rows * intersection_atm.shape[2] * fields
+    halo = (rows + 2, cells + 2 * EDGE, channels)
+    spread = (3, rows + 2, cells, channels)
+    small = 2 * fields
+
+    def pair(count):
+        return (pltpu.SemaphoreType.DMA((count,)), pltpu.SemaphoreType.DMA((count,)))
+
+    vmem = pl.BlockSpec(memory_space=pltpu.VMEM)
+    smem = pl.BlockSpec(memory_space=pltpu.SMEM)
+    scratch = [
+        pltpu.VMEM(halo, BF16),
+        pltpu.VMEM(halo, BF16),
+        pltpu.VMEM(halo, F32),
+        pltpu.VMEM(spread, BF16),
+        pltpu.VMEM((3, channels, (rows + 2) * cells), BF16),
+        pltpu.VMEM(spread, BF16),
+        pltpu.VMEM((entries, cells), jnp.int32),
+        pltpu.VMEM((entries, cells), jnp.int32),
+        pltpu.VMEM((tiles, rows * fields, cells), F32),
+        pltpu.VMEM((tiles, rows * fields, cells), F32),
+        pltpu.VMEM((2 * rows * fields, channels), F32),
+        pltpu.VMEM((grad_rows, channels), F32),
+        pltpu.VMEM((grad_rows, channels), BF16),
+        pltpu.VMEM((band, channels), BF16),
+        pltpu.VMEM((lon_tiles, members, sub, channels), BF16),
+        pltpu.VMEM((members, lon_tiles, sub, channels), BF16),
+        pltpu.VMEM((lon_tiles, sub, channels), BF16),
+        pltpu.VMEM((lon_tiles, sub, channels), BF16),
+        pltpu.VMEM((members, sub, channels), BF16),
+        pltpu.VMEM((lat_tiles, small, channels), F32),
+        pltpu.VMEM((members, small, channels), F32),
+        pltpu.VMEM((lon_tiles, small, channels), F32),
+        pair(5),
+        pair(5),
+        pair(tiles),
+        pair(2 * lat_tiles),
+        pair(2 * members),
+        pair(2 * lon_tiles),
+        pair(members),
+    ]
+    cost = pl.CostEstimate(
+        flops=2 * rows * cells * channels * channels * 29, bytes_accessed=3 << 20, transcendentals=rows * cells * channels
+    )
+    input_grad, weight_grads, flux_grad = pl.pallas_call(
+        functools.partial(fused_kernel, (members, lat_tiles, lon_tiles, grad_scale)),
+        out_shape=(
+            jax.ShapeDtypeStruct(state.shape, BF16),
+            jax.ShapeDtypeStruct((band // lon_tiles, channels), F32),
+            jax.ShapeDtypeStruct((fields, channels), F32),
+        ),
+        in_specs=[vmem] * 7 + [smem] * 3,
+        out_specs=(vmem, vmem, vmem),
+        scratch_shapes=scratch,
+        cost_estimate=cost,
+        compiler_params=pltpu.CompilerParams(
+            collective_id=0, has_side_effects=True, vmem_limit_bytes=48 << 20
+        ),
+    )(
+        state[0],
+        state_cot[0],
+        flux_cot[0].reshape(-1, cells),
+        conv_weight,
+        mix_weight,
+        flux_weight,
+        regrid_weights,
+        intersection_atm,
+        intersection_offset,
+        wet_rows,
+    )
+    return input_grad, weight_grads, flux_grad
+
+
+def step(state, state_cot, flux_cot, conv_weight, *rest):
+    members, lat_tiles, lon_tiles = (lax.axis_size(name) for name in ("ens", "oy", "ox"))
+    grad_rows = (conv_weight.shape[0] + 1) * state.shape[3]
+    whole_tiles = grad_rows % (lat_tiles * lon_tiles * members * EDGE) == 0
+    fused = lat_tiles == 2 and lon_tiles > 1 and whole_tiles
+    return (fused_body if fused else body)(state, state_cot, flux_cot, conv_weight, *rest)
+
+
 def solution(mesh):
     in_specs = (
         P("ens", "oy", "ox", None),
@@ -197,4 +620,4 @@
         P("oy", "ox"),
     )
     out_specs = (P("ens", "oy", "ox", None), P(("oy", "ox"), None), P())
-    return jax.shard_map(body, mesh=mesh, in_specs=in_specs, out_specs=out_specs, check_vma=False)
+    return jax.shard_map(step, mesh=mesh, in_specs=in_specs, out_specs=out_specs, check_vma=False)

time: 173 us -> 47.7 us (0.28)
  waiting for transfers between devices: 68 us -> 0 us
  blocking collectives: 41.4 us -> 0 us
  Pallas kernels: 0 us -> 35.7 us
  starting transfers between devices: 18.7 us -> 0 us
  between operations: 15.2 us -> 1.29 us
  matrix products: 13.4 us -> 0 us
  other arithmetic: 3.51 us -> 0 us
  local copies, waits for them, and re-layouts: 12.1 us -> 10.2 us
    psum x1 -> x0, waiting for transfers between devices: 44.5 us -> none  [body(): weight_out = lax.psum(weight_rows, 'ens')]
    psum x1 -> x0, blocking collectives: 41.4 us -> none  [body(): flux_total = lax.psum(flux_term, ('ens', 'oy', 'ox'))]
    pallas_call x0 -> x1, Pallas kernels: none -> 35.7 us  [fused_body(): pl.pallas_call(functools.partial(fused_kernel, (members, lat_tiles, lon_t...]
    dot_general x33 -> x0, matrix products: 13.4 us -> none  [the longest x1 4.44 us: body(): jnp.einsum('qsefa,qseoa->qsefo', picked_cot, picked_maps, preferred_eleme...]
    reduce_scatter x1 -> x0, waiting for transfers between devices: 12.3 us -> none  [body(): lax.psum_scatter(weight_term, ('oy', 'ox'), scatter_dimension=0, tiled=True)]
    all_to_all x2 -> x0, starting transfers between devices: 9.56 us -> none  [the longest x1 6.3 us: body(): lax.all_to_all(outbound[1], 'ox', split_axis=0, concat_axis=0, tiled=True)]
    all_to_all x2 -> x0, waiting for transfers between devices: 9.3 us -> none  [the longest x1 5.43 us: body(): lax.all_to_all(outbound[0], 'ox', split_axis=0, concat_axis=0, tiled=True)]
    ppermute x9 -> x0, starting transfers between devices: 9.05 us -> none  [the longest x4 7.6 us: with_halo(): lax.ppermute(head, axis, [((i + 1) % count, i) for i in range(count)])]
  transfers between devices with their start and end apart: 13 -> 0, of which waited for: 7 -> 0; matrix products, arithmetic and copies ran while one was open for 11% -> 0% of each run, Pallas kernels for 0% -> 0%
where the time goes in v1:
time: 47.7 us; the launch traced here: 47.3 us
  Pallas kernels  35.7 us (75%)
  local copies, waits for them, and re-layouts  10.2 us (21%)
  between operations  1.29 us (3%)
    pallas_call x1, Pallas kernels, fused_body(): pl.pallas_call(functools.partial(fused_kernel, (members, lat_tiles, lon_t...  35.7 us
    unnamed x19, local copies, waits for them, and re-layouts  10.2 us

profile of v1, /device:TPU:0, one launch (start us, length us, event | category | flops | bytes accessed | tf_op | source)
XLA Modules:
  0.0 47.3 jit_solution(16735154080585874142)
XLA Ops:
  1.3 0.8 %copy.13.atm = s32[8,4,4]{2,1,0:T(4,128)S(1)} copy(s32[8,4,4]{0,2,1:T(4,128)} %param.17) | data formatting | bytes 1024 | tf_op args[7]
  2.1 0.8 %copy.14.offset = s32[8,4,4]{2,1,0:T(4,128)S(1)} copy(s32[8,4,4]{0,2,1:T(4,128)} %param.18) | data formatting | bytes 1024 | tf_op args[8]
  2.9 0.0 copy-start
  2.9 1.3 %copy-done = bf16[9,256,256]{2,1,0:T(8,128)(2,1)S(1)} copy-done((bf16[9,256,256]{2,1,0:T(8,128)(2,1)S(1)}, bf16[9,256,256]{2,1,0:T(8,128)(2,1)}, u32[]{:S(2)}) %copy-start) | copy-done | bytes 1179672
  4.1 0.0 copy-start.1
  4.1 1.0 %copy-done.1 = bf16[16,128,128]{2,1,0:T(8,128)(2,1)S(1)} copy-done((bf16[16,128,128]{2,1,0:T(8,128)(2,1)S(1)}, bf16[16,128,128]{2,1,0:T(8,128)(2,1)}, u32[]{:S(2)}) %copy-start.1) | copy-done | bytes 524312
  5.2 0.0 copy-start.2
  5.2 0.9 %copy-done.2 = bf16[1,4,128,256]{3,2,1,0:T(8,128)(2,1)S(1)} copy-done((bf16[1,4,128,256]{3,2,1,0:T(8,128)(2,1)S(1)}, bf16[1,4,128,256]{3,2,1,0:T(8,128)(2,1)}, u32[]{:S(2)}) %copy-start.2) | copy-done | bytes 262168
  6.1 0.0 copy-start.3
  6.1 0.9 %copy-done.3 = bf16[1,4,128,256]{3,2,1,0:T(8,128)(2,1)S(1)} copy-done((bf16[1,4,128,256]{3,2,1,0:T(8,128)(2,1)S(1)}, bf16[1,4,128,256]{3,2,1,0:T(8,128)(2,1)}, u32[]{:S(2)}) %copy-start.3) | copy-done | bytes 262168
  7.1 0.0 copy-start.4
  7.1 0.9 %copy-done.4 = bf16[256,256]{1,0:T(8,128)(2,1)S(1)} copy-done((bf16[256,256]{1,0:T(8,128)(2,1)S(1)}, bf16[256,256]{1,0:T(8,128)(2,1)}, u32[]{:S(2)}) %copy-start.4) | copy-done | bytes 131096
  8.0 0.0 copy-start.5
  8.0 0.8 %copy-done.5 = bf16[1,64,4,128]{3,2,1,0:T(4,128)(2,1)S(1)} copy-done((bf16[1,64,4,128]{3,2,1,0:T(4,128)(2,1)S(1)}, bf16[1,64,4,128]{3,2,1,0:T(4,128)(2,1)}, u32[]{:S(2)}) %copy-start.5) | copy-done | bytes 65560
  8.8 0.0 copy-start.6
  8.8 0.7 %copy-done.6 = bf16[4,256]{1,0:T(4,128)(2,1)S(1)} copy-done((bf16[4,256]{1,0:T(4,128)(2,1)S(1)}, bf16[4,256]{1,0:T(4,128)(2,1)}, u32[]{:S(2)}) %copy-start.6) | copy-done | bytes 2072
  9.5 35.7 %shard_map.121 = (bf16[1,4,128,256]{3,2,1,0:T(8,128)(2,1)S(1)}, f32[320,256]{1,0:T(8,128)S(1)}, f32[4,256]{1,0:T(4,128)S(1)}) custom-call(bf16[4,128,256]{2,1,0:T(8,128)(2,1)S(1)} %bitcast.3, bf16[4,128,256]{2,1,0:T(8,128)(2,1)S(1)} %bitcast.4, bf16[256,128]{1,0:T(8,128)(2,1)S(1)} %bitcast.5, bf16[9,256,256]{2,1,0:T(8,128)(2,1)S(1)} %copy-done, ...), custom_call_target="tpu_custom_call" | custom-call | flops 1946157056 | bytes 3145728 | tf_op jit(solution)/shard_map/pallas_call | solution.py:572
  45.2 0.7 %copy.19 = bf16[1,4,128,256]{3,2,1,0:T(8,128)(2,1)} copy(bf16[1,4,128,256]{3,2,1,0:T(8,128)(2,1)S(1)} %get-tuple-element.6) | data formatting | bytes 524288
  45.9 0.7 %copy.20 = f32[320,256]{1,0:T(8,128)} copy(f32[320,256]{1,0:T(8,128)S(1)} %get-tuple-element.7) | data formatting | bytes 655360
  46.7 0.6 %copy.21 = f32[4,256]{1,0:T(4,128)} copy(f32[4,256]{1,0:T(4,128)S(1)} %get-tuple-element.8) | data formatting | bytes 8192
Async XLA Ops:
  2.9 1.3 %copy-start = (bf16[9,256,256]{2,1,0:T(8,128)(2,1)S(1)}, bf16[9,256,256]{2,1,0:T(8,128)(2,1)}, u32[]{:S(2)}) copy-start(bf16[9,256,256]{2,1,0:T(8,128)(2,1)} %conv.1) | copy-start | bytes 3538948
  4.1 1.0 %copy-start.1 = (bf16[16,128,128]{2,1,0:T(8,128)(2,1)S(1)}, bf16[16,128,128]{2,1,0:T(8,128)(2,1)}, u32[]{:S(2)}) copy-start(bf16[16,128,128]{2,1,0:T(8,128)(2,1)} %regrid.1) | copy-start | bytes 1572868
  5.2 0.9 %copy-start.2 = (bf16[1,4,128,256]{3,2,1,0:T(8,128)(2,1)S(1)}, bf16[1,4,128,256]{3,2,1,0:T(8,128)(2,1)}, u32[]{:S(2)}) copy-start(bf16[1,4,128,256]{3,2,1,0:T(8,128)(2,1)} %param.10) | copy-start | bytes 786436
  6.1 0.9 %copy-start.3 = (bf16[1,4,128,256]{3,2,1,0:T(8,128)(2,1)S(1)}, bf16[1,4,128,256]{3,2,1,0:T(8,128)(2,1)}, u32[]{:S(2)}) copy-start(bf16[1,4,128,256]{3,2,1,0:T(8,128)(2,1)} %param.11) | copy-start | bytes 786436
  7.1 0.9 %copy-start.4 = (bf16[256,256]{1,0:T(8,128)(2,1)S(1)}, bf16[256,256]{1,0:T(8,128)(2,1)}, u32[]{:S(2)}) copy-start(bf16[256,256]{1,0:T(8,128)(2,1)} %mix.1) | copy-start | bytes 393220
  8.0 0.8 %copy-start.5 = (bf16[1,64,4,128]{3,2,1,0:T(4,128)(2,1)S(1)}, bf16[1,64,4,128]{3,2,1,0:T(4,128)(2,1)}, u32[]{:S(2)}) copy-start(bf16[1,64,4,128]{3,2,1,0:T(4,128)(2,1)} %param.12) | copy-start | bytes 196612
  8.8 0.7 %copy-start.6 = (bf16[4,256]{1,0:T(4,128)(2,1)S(1)}, bf16[4,256]{1,0:T(4,128)(2,1)}, u32[]{:S(2)}) copy-start(bf16[4,256]{1,0:T(4,128)(2,1)} %flux_weight.1) | copy-start | bytes 6148

commit v2 on v1

--- a/solution.py
+++ b/solution.py
@@ -248,16 +248,51 @@
     return copies
 
 
-def shift_cells(padded, wide, shifts, rows, cells):
+def wait_all(copies):
+    for copy in copies:
+        copy.wait_recv()
+
+
+def shift_cells(padded, wide, columns, rows, cells, order):
+    channels = padded.shape[2]
     for row in range(rows + 2):
         wide[row] = padded[row].astype(F32)
-        for col in range(3):
-            shifts[col, row] = wide[row, pl.ds(EDGE - 1 + col, cells), :].astype(BF16)
+        for n, col in enumerate(order):
+            here = slice(n * channels, (n + 1) * channels)
+            if col == 1:
+                columns[row, :, here] = padded[row, EDGE : EDGE + cells]
+            else:
+                columns[row, :, here] = wide[row, pl.ds(EDGE - 1 + col, cells), :].astype(BF16)
+
+
+def store_rows(target, first, value):
+    pieces, sub = target.shape[1:3]
+    done = 0
+    while done < value.shape[0]:
+        at = first + done
+        piece, row = at // sub, at % sub
+        count = min(sub - row, value.shape[0] - done)
+        target[piece // pieces, piece % pieces, row : row + count, :] = value[done : done + count].astype(
+            target.dtype
+        )
+        done += count
 
 
 def fused_kernel(
     sizes,
-    state,
+    state_in,
+    cot_in,
+    flux_cot_in,
+    conv_in,
+    mix_in,
+    flux_weight_in,
+    regrid_in,
+    atm_in,
+    offset_in,
+    wet,
+    input_out,
+    weight_out,
+    flux_out,
     cot,
     flux_cot,
     conv,
@@ -266,16 +301,12 @@
     regrid,
     atm,
     offset,
-    wet,
-    input_out,
-    weight_out,
-    flux_out,
     padded,
     padded_grad,
     wide,
-    shifts,
+    columns,
     turned,
-    grad_shifts,
+    grad_columns,
     entry_cell,
     entry_map,
     flux_send,
@@ -292,23 +323,27 @@
     flux_lat,
     flux_ens,
     flux_lon,
+    load_sems,
     state_sems,
     grad_sems,
     flux_sems,
+    flux_lat_sems,
+    flux_ens_sems,
+    flux_lon_sems,
     lat_sems,
     ens_sems,
     lon_sems,
     out_sems,
 ):
-    members, lat_tiles, lon_tiles, grad_scale = sizes
+    members, lat_tiles, lon_tiles, grad_scale, chunks = sizes
     ens, lat, lon = lax.axis_index("ens"), lax.axis_index("oy"), lax.axis_index("ox")
-    rows, cells, channels = state.shape
+    rows, cells, channels = cot.shape
     fields = flux_weight.shape[0]
-    intersections = atm.shape[2]
+    intersections = atm.shape[1]
     maps = regrid.shape[0]
     tiles = lat_tiles * lon_tiles
     flat = lat * lon_tiles + lon
-    blocks = flux_cot.shape[0] // fields
+    cells_here = flux_cot.shape[0]
 
     barrier = pltpu.get_barrier_semaphore()
     for step in range(1, tiles):
@@ -320,29 +355,52 @@
         pl.semaphore_signal(
             barrier, inc=1, device_id={"ens": lax.rem(ens + step, members)}, device_id_type=MESH
         )
-
-    field_iota = lax.broadcasted_iota(jnp.int32, (fields, cells), 0)
+    loads = [
+        pltpu.make_async_copy(src, dst, load_sems.at[n])
+        for n, (src, dst) in enumerate(
+            [
+                (atm_in, atm),
+                (offset_in, offset),
+                (flux_cot_in, flux_cot),
+                (regrid_in, regrid),
+                (cot_in, cot),
+                (mix_in, mix),
+                (state_in, padded.at[pl.ds(1, rows), pl.ds(EDGE, cells)]),
+                (flux_weight_in, flux_weight),
+                (conv_in, conv),
+            ]
+        )
+    ]
+    for load in loads:
+        load.start()
+
+    loads[0].wait()
+    loads[1].wait()
     entry = 0
     for k in range(intersections):
         for tile in range(tiles):
             for row in range(rows):
-                at = ((tile // lon_tiles) * rows + row, tile % lon_tiles, k)
-                block = atm[at]
-                local = jnp.where(block // blocks == flat, lax.rem(block, blocks) * fields, -fields)
-                entry_cell[pl.ds(entry, fields), :] = field_iota + local
+                at = (tile % lon_tiles, k, (tile // lon_tiles) * rows + row)
+                entry_cell[pl.ds(entry, fields), :] = jnp.full((fields, cells), atm[at], jnp.int32)
                 entry_map[pl.ds(entry, fields), :] = jnp.full((fields, cells), offset[at], jnp.int32)
                 entry += fields
-    which_cell = entry_cell[...]
+    field_iota = lax.broadcasted_iota(jnp.int32, entry_cell.shape, 0) % fields
+    lane = lax.broadcasted_iota(jnp.int32, entry_cell.shape, 1)
+    which_cell = entry_cell[...] * fields + (field_iota - lane - flat * cells_here)
     which_map = entry_map[...]
-    lane = lax.broadcasted_iota(jnp.int32, which_cell.shape, 1)
-    picked = jnp.zeros(which_cell.shape, F32)
-    for part in range(blocks * fields // cells):
-        one_hot = jnp.where(which_cell == lane + part * cells, 1.0, 0.0).astype(BF16)
-        picked = picked + dot(one_hot, flux_cot[pl.ds(part * cells, cells), :])
+    loads[2].wait()
+    one_hot = [
+        jnp.where(which_cell == part * cells, 1.0, 0.0).astype(BF16) for part in range(cells_here // cells)
+    ]
+    picked = dot(jnp.concatenate(one_hot, axis=1), flux_cot[...])
+    loads[3].wait()
     products = jnp.zeros(which_cell.shape, F32)
-    for m in range(maps):
-        chosen = jnp.where(which_map == m, picked, 0.0).astype(BF16)
-        products = products + dot(chosen, regrid[m], ((1,), (1,)))
+    for m in range(0, maps, 2):
+        chosen = [jnp.where(which_map == n, picked, 0.0).astype(BF16) for n in range(m, min(m + 2, maps))]
+        taken = [regrid[n] for n in range(m, min(m + 2, maps))]
+        products = products + dot(
+            jnp.concatenate(chosen, axis=1), jnp.concatenate(taken, axis=1), ((1,), (1,))
+        )
     products = products.astype(BF16).astype(F32)
     span = tiles * rows * fields
     share = products[:span]
@@ -354,14 +412,10 @@
     outside = lat * (rows + 1)
     padded[pl.ds(outside, 1)] = jnp.zeros((1,) + padded.shape[1:], BF16)
     padded_grad[pl.ds(outside, 1)] = jnp.zeros((1,) + padded.shape[1:], BF16)
-    padded[1 : rows + 1, EDGE : EDGE + cells] = state[...]
-    flux_rows[...] = jnp.zeros(flux_rows.shape, F32)
-    for n in range(2 * rows):
-        flux_rows[n * fields : (n + 1) * fields, :] = flux_weight[...].astype(F32)
 
     pl.semaphore_wait(barrier, tiles - 1 + members - 1)
     state_copies = start_all(
-        halo_copies(state, (0, 0), padded, rows, cells, lat, lon, lon_tiles, state_sems)
+        halo_copies(state_in, (0, 0), padded, rows, cells, lat, lon, lon_tiles, state_sems)
     )
     flux_copies = []
     for step in range(1, tiles):
@@ -377,23 +431,30 @@
         )
     start_all(flux_copies)
 
+    for load in loads[4:]:
+        load.wait()
+    flux_rows[...] = jnp.zeros(flux_rows.shape, F32)
+    for n in range(2 * rows):
+        flux_rows[n * fields : (n + 1) * fields, :] = flux_weight[...].astype(F32)
     cot_flat = cot[...].reshape(rows * cells, channels)
     act_grad = dot(cot_flat, mix[...], ((1,), (1,)))
-    for copy in state_copies:
-        copy.wait_recv()
-    shift_cells(padded, wide, shifts, rows, cells)
+    wait_all(state_copies)
+    shift_cells(padded, wide, columns, rows, cells, (0, 1, 2))
     hidden = jnp.zeros((rows * cells, channels), F32)
-    for tap in range(9):
-        p, q = tap // 3, tap % 3
-        hidden = hidden + dot(shifts[q, p : p + rows].reshape(rows * cells, channels), conv[tap])
+    for p in range(3):
+        hidden = hidden + dot(
+            columns[p : p + rows].reshape(rows * cells, 3 * channels),
+            conv[3 * p : 3 * p + 3].reshape(3 * channels, channels),
+        )
     gate = jax.nn.sigmoid(hidden)
     activation = (hidden * gate).astype(BF16)
     slope = gate * (1.0 + hidden * (1.0 - gate))
-    for q in range(3):
-        turned[q] = shifts[q].reshape((rows + 2) * cells, channels).T
-
-    for copy in flux_copies:
-        copy.wait_recv()
+    turned[...] = columns[...].reshape((rows + 2) * cells, 3 * channels).T
+    term = dot(activation, cot_flat, ((0,), (0,)))
+    store_rows(grads, 9 * channels, term)
+    store_rows(grads_half, 9 * channels, term)
+
+    wait_all(flux_copies)
     row_iota = lax.broadcasted_iota(jnp.int32, (rows * fields, cells), 0) // fields
     flux = flux_recv[0]
     for tile in range(1, tiles):
@@ -404,104 +465,174 @@
     both = jnp.concatenate([flux_high, flux_low], axis=0)
     both_iota = jnp.concatenate([row_iota, row_iota], axis=0)
     heads = flux_rows[...].astype(BF16)
-    flux_term = jnp.zeros((2 * rows * fields, channels), F32)
+    masked = []
     for row in range(rows):
         mine = jnp.where(both_iota == row, both, 0.0).astype(BF16)
+        masked.append(mine)
         here = slice(row * cells, (row + 1) * cells)
         extra = dot(mine, heads, ((0,), (0,)))
-        grad = ((act_grad[here] + extra) * slope[here]).astype(BF16)
-        padded_grad[row + 1, EDGE : EDGE + cells] = grad
-        flux_term = flux_term + dot(mine, activation[here])
+        padded_grad[row + 1, EDGE : EDGE + cells] = ((act_grad[here] + extra) * slope[here]).astype(BF16)
     grad_copies = start_all(
         halo_copies(padded_grad, (1, EDGE), padded_grad, rows, cells, lat, lon, lon_tiles, grad_sems)
     )
 
-    flux_rows[...] = flux_term
+    hidden_grad = padded_grad[1 : rows + 1, EDGE : EDGE + cells].reshape(rows * cells, channels)
+    for p in range(3):
+        term = dot(turned[:, p * cells : (p + rows) * cells], hidden_grad)
+        store_rows(grads, 3 * p * channels, term)
+        store_rows(grads_half, 3 * p * channels, term)
+
+    lat_copies = [
+        start_all(
+            exchange(
+                "oy",
+                lat_tiles,
+                lat,
+                lambda to: grads_half.at[to, :, pl.ds(at, count)],
+                lambda me: recv_lat.at[:, pl.ds(at, count)],
+                lat_sems,
+                n * lat_tiles,
+            )
+        )
+        for n, (at, count) in enumerate(chunks)
+    ]
+    flux_rows[...] = dot(jnp.concatenate(masked, axis=1), activation)
     total = flux_rows[:fields, :]
     for n in range(1, 2 * rows):
         total = total + flux_rows[n * fields : (n + 1) * fields, :]
     flux_lat[pl.ds(lat, 1)] = jnp.zeros((1,) + flux_lat.shape[1:], F32)
     flux_lat[pl.ds(lat, 1), 0:fields, :] = total[None]
-
-    hidden_grad = padded_grad[1 : rows + 1, EDGE : EDGE + cells].reshape(rows * cells, channels)
-    for tap in range(10):
-        p, q = tap // 3, tap % 3
-        if tap < 9:
-            term = dot(turned[q, :, p * cells : (p + rows) * cells], hidden_grad)
-        else:
-            term = dot(activation, cot_flat, ((0,), (0,)))
-        grads[tap * channels : (tap + 1) * channels, :] = term
-        grads_half[tap * channels : (tap + 1) * channels, :] = term.astype(BF16)
-
-    band = grads.shape[0] // lat_tiles
-    lat_copies = start_all(
-        exchange(
-            "oy",
-            lat_tiles,
-            lat,
-            lambda to: grads_half.at[pl.ds(pl.multiple_of(to * band, band), band)],
-            lambda me: recv_lat,
-            lat_sems,
-        )
-        + exchange("oy", lat_tiles, lat, lambda to: flux_lat.at[lat], lambda me: flux_lat.at[me], lat_sems, lat_tiles)
-    )
-    for copy in lat_copies:
-        copy.wait_recv()
-    own = grads[pl.ds(pl.multiple_of(lat * band, band), band), :]
-    sum_lat[...] = (own + recv_lat[...].astype(F32)).astype(BF16).reshape(sum_lat.shape)
+    flux_lat_copies = start_all(
+        exchange("oy", lat_tiles, lat, lambda to: flux_lat.at[lat], lambda me: flux_lat.at[me], flux_lat_sems)
+    )
+
+    ens_copies = []
+    for n, (at, count) in enumerate(chunks):
+        wait_all(lat_copies[n])
+        own = grads[pl.ds(lat, 1), :, at : at + count]
+        part = (own[0] + recv_lat[:, at : at + count].astype(F32)).astype(BF16)
+        sum_lat[:, :, at : at + count] = part.reshape(lon_tiles, members, count, channels)
+        ens_copies.append(
+            start_all(
+                exchange(
+                    "ens",
+                    members,
+                    ens,
+                    lambda to: sum_lat.at[:, to, pl.ds(at, count)],
+                    lambda me: recv_ens.at[me, :, pl.ds(at, count)],
+                    ens_sems,
+                    n * members,
+                )
+            )
+        )
+    recv_ens[pl.ds(ens, 1)] = sum_lat[:, pl.ds(ens, 1)].reshape((1,) + recv_ens.shape[1:])
+    wait_all(flux_lat_copies)
     total = flux_lat[0]
     for n in range(1, lat_tiles):
         total = total + flux_lat[n]
     flux_ens[pl.ds(ens, 1)] = total[None]
-    ens_copies = start_all(
-        exchange("ens", members, ens, lambda to: sum_lat.at[:, to], lambda me: recv_ens.at[me], ens_sems)
-        + exchange("ens", members, ens, lambda to: flux_ens.at[ens], lambda me: flux_ens.at[me], ens_sems, members)
-    )
-    recv_ens[pl.ds(ens, 1)] = sum_lat[:, pl.ds(ens, 1)].reshape((1,) + recv_ens.shape[1:])
-
-    for copy in grad_copies:
-        copy.wait_recv()
-    shift_cells(padded_grad, wide, grad_shifts, rows, cells)
+    flux_ens_copies = start_all(
+        exchange("ens", members, ens, lambda to: flux_ens.at[ens], lambda me: flux_ens.at[me], flux_ens_sems)
+    )
+
+    wait_all(grad_copies)
+    shift_cells(padded_grad, wide, grad_columns, rows, cells, (2, 1, 0))
     input_grad = cot_flat.astype(F32)
-    for tap in range(9):
-        p, q = tap // 3, tap % 3
-        back = grad_shifts[2 - q, 2 - p : 2 - p + rows].reshape(rows * cells, channels)
-        input_grad = input_grad + dot(back, conv[tap], ((1,), (1,)))
+    for p in range(3):
+        back = grad_columns[2 - p : 2 - p + rows].reshape(rows * cells, 3 * channels)
+        taps = jnp.concatenate([conv[3 * p + q] for q in range(3)], axis=1)
+        input_grad = input_grad + dot(back, taps, ((1,), (1,)))
     input_out[...] = input_grad.astype(BF16).reshape(input_out.shape)
 
-    for copy in ens_copies:
-        copy.wait_recv()
-    total = recv_ens[0].astype(F32)
-    for n in range(1, members):
-        total = total + recv_ens[n].astype(F32)
-    sum_ens[...] = total.astype(BF16)
-    total = flux_ens[0]
-    for n in range(1, members):
-        total = total + flux_ens[n]
-    flux_lon[pl.ds(lon, 1)] = total[None]
-    lon_copies = start_all(
-        exchange("ox", lon_tiles, lon, lambda to: sum_ens.at[to], lambda me: recv_lon.at[me], lon_sems)
-        + exchange("ox", lon_tiles, lon, lambda to: flux_lon.at[lon], lambda me: flux_lon.at[me], lon_sems, lon_tiles)
-    )
-    recv_lon[pl.ds(lon, 1)] = sum_ens[pl.ds(lon, 1)]
-    for copy in lon_copies:
-        copy.wait_recv()
-    total = recv_lon[0].astype(F32)
-    for n in range(1, lon_tiles):
-        total = total + recv_lon[n].astype(F32)
-    rows_all[pl.ds(ens, 1)] = (total * grad_scale).astype(BF16)[None]
-    out_copies = start_all(
-        exchange("ens", members, ens, lambda to: rows_all.at[ens], lambda me: rows_all.at[me], out_sems)
-    )
+    lon_copies, out_copies = [], []
+
+    def gather_chunk(n):
+        at, count = chunks[n]
+        wait_all(lon_copies[n])
+        total = recv_lon[0, at : at + count].astype(F32)
+        for other in range(1, lon_tiles):
+            total = total + recv_lon[other, at : at + count].astype(F32)
+        rows_all[pl.ds(ens, 1), at : at + count] = (total * grad_scale).astype(BF16)[None]
+        out_copies.append(
+            start_all(
+                exchange(
+                    "ens",
+                    members,
+                    ens,
+                    lambda to: rows_all.at[ens, pl.ds(at, count)],
+                    lambda me: rows_all.at[me, pl.ds(at, count)],
+                    out_sems,
+                    n * members,
+                )
+            )
+        )
+
+    for n, (at, count) in enumerate(chunks):
+        wait_all(ens_copies[n])
+        total = recv_ens[0, :, at : at + count].astype(F32)
+        for other in range(1, members):
+            total = total + recv_ens[other, :, at : at + count].astype(F32)
+        sum_ens[:, at : at + count] = total.astype(BF16)
+        lon_copies.append(
+            start_all(
+                exchange(
+                    "ox",
+                    lon_tiles,
+                    lon,
+                    lambda to: sum_ens.at[to, pl.ds(at, count)],
+                    lambda me: recv_lon.at[me, pl.ds(at, count)],
+                    lon_sems,
+                    n * lon_tiles,
+                )
+            )
+        )
+        recv_lon[pl.ds(lon, 1), at : at + count] = sum_ens[pl.ds(lon, 1), at : at + count]
+        if n == 0:
+            wait_all(flux_ens_copies)
+            total = flux_ens[0]
+            for other in range(1, members):
+                total = total + flux_ens[other]
+            flux_lon[pl.ds(lon, 1)] = total[None]
+            flux_lon_copies = start_all(
+                exchange("ox", lon_tiles, lon, lambda to: flux_lon.at[lon], lambda me: flux_lon.at[me], flux_lon_sems)
+            )
+        else:
+            gather_chunk(n - 1)
+    wait_all(flux_lon_copies)
     total = flux_lon[0]
     for n in range(1, lon_tiles):
         total = total + flux_lon[n]
     flux_out[...] = total[:fields] * grad_scale
-    for copy in out_copies:
-        copy.wait_recv()
+    gather_chunk(len(chunks) - 1)
+    for copies in out_copies:
+        wait_all(copies)
     weight_out[...] = rows_all[...].astype(F32).reshape(weight_out.shape)
-    for copy in state_copies + flux_copies + grad_copies + lat_copies + ens_copies + lon_copies + out_copies:
-        copy.wait_send()
+    started = state_copies + flux_copies + grad_copies + flux_lat_copies + flux_ens_copies + flux_lon_copies
+    for copies in [started] + lat_copies + ens_copies + lon_copies + out_copies:
+        for copy in copies:
+            copy.wait_send()
+
+
+def place_kernel(*refs):
+    count = len(refs) // 2
+    sems = refs[-1]
+    copies = [pltpu.make_async_copy(refs[n], refs[count + n], sems.at[n]) for n in range(count)]
+    for copy in copies:
+        copy.start()
+    for copy in copies:
+        copy.wait()
+
+
+def place(arrays):
+    anywhere = pl.BlockSpec(memory_space=pl.ANY)
+    return pl.pallas_call(
+        place_kernel,
+        out_shape=tuple(jax.ShapeDtypeStruct(a.shape, a.dtype) for a in arrays),
+        in_specs=[anywhere] * len(arrays),
+        out_specs=tuple([anywhere] * len(arrays)),
+        scratch_shapes=[pltpu.SemaphoreType.DMA((len(arrays),))],
+        compiler_params=pltpu.CompilerParams(vmem_limit_bytes=60 << 20),
+    )(*arrays)
 
 
 def fused_body(
@@ -517,39 +648,52 @@
     wet_rows,
 ):
     members, lat_tiles, lon_tiles = (lax.axis_size(name) for name in ("ens", "oy", "ox"))
-    tile = state.shape[1:]
-    rows, cells, channels = tile
+    rows, cells, channels = state.shape[1:]
     fields = flux_weight.shape[0]
     tiles = lat_tiles * lon_tiles
     grad_rows = (conv_weight.shape[0] + 1) * channels
     band = grad_rows // lat_tiles
-    sub = band // lon_tiles // members
+    pieces = lon_tiles * members
+    sub = band // pieces
     grad_scale = 1.0 / math.sqrt(members * lat_tiles * rows * lon_tiles * cells)
     entries = tiles * rows * intersection_atm.shape[2] * fields
     halo = (rows + 2, cells + 2 * EDGE, channels)
-    spread = (3, rows + 2, cells, channels)
+    spread = (rows + 2, cells, 3 * channels)
     small = 2 * fields
+    size = 2 * EDGE
+    chunks = [(at, min(size, sub - at)) for at in range(0, sub, size)]
 
     def pair(count):
         return (pltpu.SemaphoreType.DMA((count,)), pltpu.SemaphoreType.DMA((count,)))
 
     vmem = pl.BlockSpec(memory_space=pltpu.VMEM)
     smem = pl.BlockSpec(memory_space=pltpu.SMEM)
+    anywhere = pl.BlockSpec(memory_space=pl.ANY)
+    flux_flat = flux_cot[0].reshape(-1, cells)
+    tables = [table.transpose(1, 2, 0) for table in (intersection_atm, intersection_offset)]
     scratch = [
+        pltpu.VMEM((rows, cells, channels), BF16),
+        pltpu.VMEM(flux_flat.shape, BF16),
+        pltpu.VMEM(conv_weight.shape, BF16),
+        pltpu.VMEM(mix_weight.shape, BF16),
+        pltpu.VMEM(flux_weight.shape, BF16),
+        pltpu.VMEM(regrid_weights.shape, BF16),
+        pltpu.SMEM(tables[0].shape, jnp.int32),
+        pltpu.SMEM(tables[1].shape, jnp.int32),
         pltpu.VMEM(halo, BF16),
         pltpu.VMEM(halo, BF16),
         pltpu.VMEM(halo, F32),
         pltpu.VMEM(spread, BF16),
-        pltpu.VMEM((3, channels, (rows + 2) * cells), BF16),
+        pltpu.VMEM((3 * channels, (rows + 2) * cells), BF16),
         pltpu.VMEM(spread, BF16),
         pltpu.VMEM((entries, cells), jnp.int32),
         pltpu.VMEM((entries, cells), jnp.int32),
         pltpu.VMEM((tiles, rows * fields, cells), F32),
         pltpu.VMEM((tiles, rows * fields, cells), F32),
         pltpu.VMEM((2 * rows * fields, channels), F32),
-        pltpu.VMEM((grad_rows, channels), F32),
-        pltpu.VMEM((grad_rows, channels), BF16),
-        pltpu.VMEM((band, channels), BF16),
+        pltpu.VMEM((lat_tiles, pieces, sub, channels), F32),
+        pltpu.VMEM((lat_tiles, pieces, sub, channels), BF16),
+        pltpu.VMEM((pieces, sub, channels), BF16),
         pltpu.VMEM((lon_tiles, members, sub, channels), BF16),
         pltpu.VMEM((members, lon_tiles, sub, channels), BF16),
         pltpu.VMEM((lon_tiles, sub, channels), BF16),
@@ -558,44 +702,48 @@
         pltpu.VMEM((lat_tiles, small, channels), F32),
         pltpu.VMEM((members, small, channels), F32),
         pltpu.VMEM((lon_tiles, small, channels), F32),
+        pltpu.SemaphoreType.DMA((9,)),
         pair(5),
         pair(5),
         pair(tiles),
-        pair(2 * lat_tiles),
-        pair(2 * members),
-        pair(2 * lon_tiles),
+        pair(lat_tiles),
         pair(members),
+        pair(lon_tiles),
+        pair(len(chunks) * lat_tiles),
+        pair(len(chunks) * members),
+        pair(len(chunks) * lon_tiles),
+        pair(len(chunks) * members),
     ]
     cost = pl.CostEstimate(
         flops=2 * rows * cells * channels * channels * 29, bytes_accessed=3 << 20, transcendentals=rows * cells * channels
     )
-    input_grad, weight_grads, flux_grad = pl.pallas_call(
-        functools.partial(fused_kernel, (members, lat_tiles, lon_tiles, grad_scale)),
+    outs = pl.pallas_call(
+        functools.partial(fused_kernel, (members, lat_tiles, lon_tiles, grad_scale, chunks)),
         out_shape=(
             jax.ShapeDtypeStruct(state.shape, BF16),
             jax.ShapeDtypeStruct((band // lon_tiles, channels), F32),
             jax.ShapeDtypeStruct((fields, channels), F32),
         ),
-        in_specs=[vmem] * 7 + [smem] * 3,
+        in_specs=[anywhere] * 9 + [smem],
         out_specs=(vmem, vmem, vmem),
         scratch_shapes=scratch,
         cost_estimate=cost,
         compiler_params=pltpu.CompilerParams(
-            collective_id=0, has_side_effects=True, vmem_limit_bytes=48 << 20
+            collective_id=0, has_side_effects=True, vmem_limit_bytes=56 << 20
         ),
     )(
         state[0],
         state_cot[0],
-        flux_cot[0].reshape(-1, cells),
+        flux_flat,
         conv_weight,
         mix_weight,
         flux_weight,
         regrid_weights,
-        intersection_atm,
-        intersection_offset,
+        tables[0],
+        tables[1],
         wet_rows,
     )
-    return input_grad, weight_grads, flux_grad
+    return place(outs)
 
 
 def step(state, state_cot, flux_cot, conv_weight, *rest):

time: 47.7 us -> 55.2 us (1.16)
  Pallas kernels: 35.7 us -> 53.7 us
  local copies, waits for them, and re-layouts: 10.2 us -> 0 us
    pallas_call x0 -> x1, Pallas kernels: none -> 19.1 us  [place(): pl.pallas_call(place_kernel, out_shape=tuple((jax.ShapeDtypeStruct(a.shap...]
    unnamed x19 -> x0, local copies, waits for them, and re-layouts: 10.2 us -> none
    pallas_call x1, Pallas kernels: 35.7 us -> 34.6 us  [fused_body(): pl.pallas_call(functools.partial(fused_kernel, (members, lat_tiles, lon_t...]
where the time goes in v2:
time: 55.2 us; the launch traced here: 55 us
  Pallas kernels  53.7 us (97%)
  between operations  1.29 us (2%)
    pallas_call x1, Pallas kernels, fused_body(): pl.pallas_call(functools.partial(fused_kernel, (members, lat_tiles, lon_t...  34.6 us
    pallas_call x1, Pallas kernels, place(): pl.pallas_call(place_kernel, out_shape=tuple((jax.ShapeDtypeStruct(a.shap...  19.1 us

profile of v2, /device:TPU:0, one launch (start us, length us, event | category | flops | bytes accessed | tf_op | source)
XLA Modules:
  0.0 55.0 jit_solution(10809683792978212538)
XLA Ops:
  1.3 34.6 %shard_map.121 = (bf16[1,4,128,256]{3,2,1,0:T(8,128)(2,1)}, f32[320,256]{1,0:T(8,128)}, f32[4,256]{1,0:T(4,128)}) custom-call(bf16[4,128,256]{2,1,0:T(8,128)(2,1)} %bitcast.5, bf16[4,128,256]{2,1,0:T(8,128)(2,1)} %bitcast.6, bf16[256,128]{1,0:T(8,128)(2,1)} %bitcast.7, bf16[9,256,256]{2,1,0:T(8,128)(2,1)} %conv_in.1, bf16[256,256]{1,0:T(8,128)(2,1)} %mix_in.1, ...), custom_call_target="tpu_custom_call" | custom-call | flops 1946157056 | bytes 3145728 | tf_op jit(solution)/shard_map/pallas_call | solution.py:720
  35.9 19.1 %shard_map.122 = (bf16[1,4,128,256]{3,2,1,0:T(8,128)(2,1)}, f32[320,256]{1,0:T(8,128)}, f32[4,256]{1,0:T(4,128)}) custom-call(bf16[1,4,128,256]{3,2,1,0:T(8,128)(2,1)} %get-tuple-element.6.refs_0_, f32[320,256]{1,0:T(8,128)} %get-tuple-element.7.refs_1_, f32[4,256]{1,0:T(4,128)} %get-tuple-element.8.refs_2_), custom_call_target="tpu_custom_call" | custom-call | tf_op jit(solution)/shard_map/pallas_call | solution.py:628

commit v3 on v2

--- a/solution.py
+++ b/solution.py
@@ -606,33 +606,44 @@
     gather_chunk(len(chunks) - 1)
     for copies in out_copies:
         wait_all(copies)
-    weight_out[...] = rows_all[...].astype(F32).reshape(weight_out.shape)
+    weight_out[...] = rows_all[...]
     started = state_copies + flux_copies + grad_copies + flux_lat_copies + flux_ens_copies + flux_lon_copies
     for copies in [started] + lat_copies + ens_copies + lon_copies + out_copies:
         for copy in copies:
             copy.wait_send()
 
 
-def place_kernel(*refs):
-    count = len(refs) // 2
-    sems = refs[-1]
-    copies = [pltpu.make_async_copy(refs[n], refs[count + n], sems.at[n]) for n in range(count)]
-    for copy in copies:
-        copy.start()
+def place_kernel(input_grad, weight_rows, flux_grad, input_out, weight_out, flux_out, wide, sems):
+    copies = [
+        pltpu.make_async_copy(input_grad, input_out, sems.at[0]),
+        pltpu.make_async_copy(flux_grad, flux_out, sems.at[1]),
+        pltpu.make_async_copy(wide, weight_out, sems.at[2]),
+    ]
+    copies[0].start()
+    copies[1].start()
+    wide[...] = weight_rows[...].reshape(wide.shape).astype(F32)
+    copies[2].start()
     for copy in copies:
         copy.wait()
 
 
-def place(arrays):
-    anywhere = pl.BlockSpec(memory_space=pl.ANY)
+def place(input_grad, weight_rows, flux_grad):
+    channels = weight_rows.shape[2]
+    weight_shape = (weight_rows.shape[0] * weight_rows.shape[1], channels)
+    vmem = pl.BlockSpec(memory_space=pltpu.VMEM)
+    hbm = pl.BlockSpec(memory_space=pltpu.HBM)
     return pl.pallas_call(
         place_kernel,
-        out_shape=tuple(jax.ShapeDtypeStruct(a.shape, a.dtype) for a in arrays),
-        in_specs=[anywhere] * len(arrays),
-        out_specs=tuple([anywhere] * len(arrays)),
-        scratch_shapes=[pltpu.SemaphoreType.DMA((len(arrays),))],
-        compiler_params=pltpu.CompilerParams(vmem_limit_bytes=60 << 20),
-    )(*arrays)
+        out_shape=(
+            jax.ShapeDtypeStruct(input_grad.shape, BF16),
+            jax.ShapeDtypeStruct(weight_shape, F32),
+            jax.ShapeDtypeStruct(flux_grad.shape, F32),
+        ),
+        in_specs=[vmem] * 3,
+        out_specs=(hbm, hbm, hbm),
+        scratch_shapes=[pltpu.VMEM(weight_shape, F32), pltpu.SemaphoreType.DMA((3,))],
+        compiler_params=pltpu.CompilerParams(vmem_limit_bytes=56 << 20),
+    )(input_grad, weight_rows, flux_grad)
 
 
 def fused_body(
@@ -668,7 +679,7 @@
 
     vmem = pl.BlockSpec(memory_space=pltpu.VMEM)
     smem = pl.BlockSpec(memory_space=pltpu.SMEM)
-    anywhere = pl.BlockSpec(memory_space=pl.ANY)
+    hbm = pl.BlockSpec(memory_space=pltpu.HBM)
     flux_flat = flux_cot[0].reshape(-1, cells)
     tables = [table.transpose(1, 2, 0) for table in (intersection_atm, intersection_offset)]
     scratch = [
@@ -721,10 +732,10 @@
         functools.partial(fused_kernel, (members, lat_tiles, lon_tiles, grad_scale, chunks)),
         out_shape=(
             jax.ShapeDtypeStruct(state.shape, BF16),
-            jax.ShapeDtypeStruct((band // lon_tiles, channels), F32),
+            jax.ShapeDtypeStruct((members, sub, channels), BF16),
             jax.ShapeDtypeStruct((fields, channels), F32),
         ),
-        in_specs=[anywhere] * 9 + [smem],
+        in_specs=[hbm] * 9 + [smem],
         out_specs=(vmem, vmem, vmem),
         scratch_shapes=scratch,
         cost_estimate=cost,
@@ -743,7 +754,7 @@
         tables[1],
         wet_rows,
     )
-    return place(outs)
+    return place(*outs)
 
 
 def step(state, state_cot, flux_cot, conv_weight, *rest):

time: 55.2 us -> 37.9 us (0.69)
  Pallas kernels: 53.7 us -> 36.4 us
    pallas_call x1, Pallas kernels: 19.1 us -> 1.88 us  [place(): pl.pallas_call(place_kernel, out_shape=(jax.ShapeDtypeStruct(input_grad.s...]
where the time goes in v3:
time: 37.9 us; the launch traced here: 37.7 us
  Pallas kernels  36.4 us (96%)
  between operations  1.29 us (3%)
    pallas_call x1, Pallas kernels, fused_body(): pl.pallas_call(functools.partial(fused_kernel, (members, lat_tiles, lon_t...  34.5 us
    pallas_call x1, Pallas kernels, place(): pl.pallas_call(place_kernel, out_shape=(jax.ShapeDtypeStruct(input_grad.s...  1.88 us

profile of v3, /device:TPU:0, one launch (start us, length us, event | category | flops | bytes accessed | tf_op | source)
XLA Modules:
  0.0 37.7 jit_solution(11363307115367603947)
XLA Ops:
  1.3 34.5 %shard_map.121 = (bf16[1,4,128,256]{3,2,1,0:T(8,128)(2,1)}, bf16[4,80,256]{2,1,0:T(8,128)(2,1)}, f32[4,256]{1,0:T(4,128)}) custom-call(bf16[4,128,256]{2,1,0:T(8,128)(2,1)} %bitcast.5, bf16[4,128,256]{2,1,0:T(8,128)(2,1)} %bitcast.6, bf16[256,128]{1,0:T(8,128)(2,1)} %bitcast.7, bf16[9,256,256]{2,1,0:T(8,128)(2,1)} %conv_in.1, bf16[256,256]{1,0:T(8,128)(2,1)} %mix_in.1, ...), custom_call_target="tpu_custom_call" | custom-call | flops 1946157056 | bytes 3145728 | tf_op jit(solution)/shard_map/pallas_call | solution.py:731
  35.8 1.9 %shard_map.122 = (bf16[1,4,128,256]{3,2,1,0:T(8,128)(2,1)}, f32[320,256]{1,0:T(8,128)}, f32[4,256]{1,0:T(4,128)}) custom-call(bf16[1,4,128,256]{3,2,1,0:T(8,128)(2,1)} %get-tuple-element.6.input_grad, bf16[4,80,256]{2,1,0:T(8,128)(2,1)} %get-tuple-element.7.weight_rows, f32[4,256]{1,0:T(4,128)} %get-tuple-element.8.flux_grad), custom_call_target="tpu_custom_call" | custom-call | tf_op jit(solution)/shard_map/pallas_call | solution.py:635

commit v4 on v3

--- a/solution.py
+++ b/solution.py
@@ -374,6 +374,15 @@
     for load in loads:
         load.start()
 
+    outside = lat * (rows + 1)
+    padded[pl.ds(outside, 1)] = jnp.zeros((1,) + padded.shape[1:], BF16)
+    padded_grad[pl.ds(outside, 1)] = jnp.zeros((1,) + padded.shape[1:], BF16)
+
+    pl.semaphore_wait(barrier, tiles - 1 + members - 1)
+    state_copies = start_all(
+        halo_copies(state_in, (0, 0), padded, rows, cells, lat, lon, lon_tiles, state_sems)
+    )
+
     loads[0].wait()
     loads[1].wait()
     entry = 0
@@ -409,14 +418,6 @@
     flux_send[...] = share.reshape(flux_send.shape)
     flux_recv[pl.ds(flat, 1)] = flux_send[pl.ds(flat, 1)]
 
-    outside = lat * (rows + 1)
-    padded[pl.ds(outside, 1)] = jnp.zeros((1,) + padded.shape[1:], BF16)
-    padded_grad[pl.ds(outside, 1)] = jnp.zeros((1,) + padded.shape[1:], BF16)
-
-    pl.semaphore_wait(barrier, tiles - 1 + members - 1)
-    state_copies = start_all(
-        halo_copies(state_in, (0, 0), padded, rows, cells, lat, lon, lon_tiles, state_sems)
-    )
     flux_copies = []
     for step in range(1, tiles):
         peer = lax.rem(flat + step, tiles)
@@ -476,11 +477,22 @@
         halo_copies(padded_grad, (1, EDGE), padded_grad, rows, cells, lat, lon, lon_tiles, grad_sems)
     )
 
-    hidden_grad = padded_grad[1 : rows + 1, EDGE : EDGE + cells].reshape(rows * cells, channels)
-    for p in range(3):
-        term = dot(turned[:, p * cells : (p + rows) * cells], hidden_grad)
-        store_rows(grads, 3 * p * channels, term)
-        store_rows(grads_half, 3 * p * channels, term)
+    def tap_grads(target, first, last):
+        hidden_grad = padded_grad[1 : rows + 1, EDGE : EDGE + cells].reshape(rows * cells, channels)
+        tap = first
+        while tap < last:
+            p, q = tap // 3, tap % 3
+            count = min(3 - q, last - tap)
+            left = turned[q * channels : (q + count) * channels, p * cells : (p + rows) * cells]
+            store_rows(target, tap * channels, dot(left, hidden_grad))
+            tap += count
+
+    taps = grads.shape[1] * grads.shape[2] // channels
+    for part in range(lat_tiles):
+
+        @pl.when(lat != part)
+        def _():
+            tap_grads(grads_half, part * taps, min((part + 1) * taps, 9))
 
     lat_copies = [
         start_all(
@@ -505,6 +517,12 @@
     flux_lat_copies = start_all(
         exchange("oy", lat_tiles, lat, lambda to: flux_lat.at[lat], lambda me: flux_lat.at[me], flux_lat_sems)
     )
+
+    for part in range(lat_tiles):
+
+        @pl.when(lat == part)
+        def _():
+            tap_grads(grads, part * taps, min((part + 1) * taps, 9))
 
     ens_copies = []
     for n, (at, count) in enumerate(chunks):
@@ -761,7 +779,8 @@
     members, lat_tiles, lon_tiles = (lax.axis_size(name) for name in ("ens", "oy", "ox"))
     grad_rows = (conv_weight.shape[0] + 1) * state.shape[3]
     whole_tiles = grad_rows % (lat_tiles * lon_tiles * members * EDGE) == 0
-    fused = lat_tiles == 2 and lon_tiles > 1 and whole_tiles
+    whole_taps = grad_rows // lat_tiles % state.shape[3] == 0
+    fused = lat_tiles == 2 and lon_tiles > 1 and whole_tiles and whole_taps
     return (fused_body if fused else body)(state, state_cot, flux_cot, conv_weight, *rest)
 
 

time: 37.9 us -> 36.9 us (0.974)
  Pallas kernels: 36.4 us -> 35.5 us
    pallas_call x1, Pallas kernels: 34.5 us -> 33.6 us  [fused_body(): pl.pallas_call(functools.partial(fused_kernel, (members, lat_tiles, lon_t...]
where the time goes in v4:
time: 36.9 us; the launch traced here: 36.7 us
  Pallas kernels  35.5 us (96%)
  between operations  1.29 us (3%)
    pallas_call x1, Pallas kernels, fused_body(): pl.pallas_call(functools.partial(fused_kernel, (members, lat_tiles, lon_t...  33.6 us
    pallas_call x1, Pallas kernels, place(): pl.pallas_call(place_kernel, out_shape=(jax.ShapeDtypeStruct(input_grad.s...  1.88 us

profile of v4, /device:TPU:0, one launch (start us, length us, event | category | flops | bytes accessed | tf_op | source)
XLA Modules:
  0.0 36.7 jit_solution(2297587199192524593)
XLA Ops:
  1.3 33.6 %shard_map.121 = (bf16[1,4,128,256]{3,2,1,0:T(8,128)(2,1)}, bf16[4,80,256]{2,1,0:T(8,128)(2,1)}, f32[4,256]{1,0:T(4,128)}) custom-call(bf16[4,128,256]{2,1,0:T(8,128)(2,1)} %bitcast.5, bf16[4,128,256]{2,1,0:T(8,128)(2,1)} %bitcast.6, bf16[256,128]{1,0:T(8,128)(2,1)} %bitcast.7, bf16[9,256,256]{2,1,0:T(8,128)(2,1)} %conv_in.1, bf16[256,256]{1,0:T(8,128)(2,1)} %mix_in.1, ...), custom_call_target="tpu_custom_call" | custom-call | flops 1946157056 | bytes 3145728 | tf_op jit(solution)/shard_map/pallas_call | solution.py:749
  34.9 1.9 %shard_map.122 = (bf16[1,4,128,256]{3,2,1,0:T(8,128)(2,1)}, f32[320,256]{1,0:T(8,128)}, f32[4,256]{1,0:T(4,128)}) custom-call(bf16[1,4,128,256]{3,2,1,0:T(8,128)(2,1)} %get-tuple-element.6.input_grad, bf16[4,80,256]{2,1,0:T(8,128)(2,1)} %get-tuple-element.7.weight_rows, f32[4,256]{1,0:T(4,128)} %get-tuple-element.8.flux_grad), custom_call_target="tpu_custom_call" | custom-call | tf_op jit(solution)/shard_map/pallas_call | solution.py:653

commit v5 on v4

--- a/solution.py
+++ b/solution.py
@@ -320,6 +320,7 @@
     sum_ens,
     recv_lon,
     rows_all,
+    input_sum,
     flux_lat,
     flux_ens,
     flux_lon,
@@ -403,18 +404,18 @@
     ]
     picked = dot(jnp.concatenate(one_hot, axis=1), flux_cot[...])
     loads[3].wait()
-    products = jnp.zeros(which_cell.shape, F32)
+    span = tiles * rows * fields
+    part_of = [slice(k * span, (k + 1) * span) for k in range(intersections)]
+    share = jnp.zeros((span, cells), F32)
     for m in range(0, maps, 2):
-        chosen = [jnp.where(which_map == n, picked, 0.0).astype(BF16) for n in range(m, min(m + 2, maps))]
-        taken = [regrid[n] for n in range(m, min(m + 2, maps))]
-        products = products + dot(
-            jnp.concatenate(chosen, axis=1), jnp.concatenate(taken, axis=1), ((1,), (1,))
-        )
-    products = products.astype(BF16).astype(F32)
-    span = tiles * rows * fields
-    share = products[:span]
-    for k in range(1, intersections):
-        share = share + products[k * span : (k + 1) * span]
+        chosen, taken = [], []
+        for n in range(m, min(m + 2, maps)):
+            total = jnp.where(which_map[part_of[0]] == n, picked[part_of[0]], 0.0)
+            for k in range(1, intersections):
+                total = total + jnp.where(which_map[part_of[k]] == n, picked[part_of[k]], 0.0)
+            chosen.append(total.astype(BF16))
+            taken.append(regrid[n])
+        share = share + dot(jnp.concatenate(chosen, axis=1), jnp.concatenate(taken, axis=1), ((1,), (1,)))
     flux_send[...] = share.reshape(flux_send.shape)
     flux_recv[pl.ds(flat, 1)] = flux_send[pl.ds(flat, 1)]
 
@@ -447,10 +448,14 @@
             columns[p : p + rows].reshape(rows * cells, 3 * channels),
             conv[3 * p : 3 * p + 3].reshape(3 * channels, channels),
         )
+        first, last = p * (rows + 2) // 3, (p + 1) * (rows + 2) // 3
+        if last > first:
+            turned[:, first * cells : last * cells] = (
+                columns[first:last].reshape((last - first) * cells, 3 * channels).T
+            )
     gate = jax.nn.sigmoid(hidden)
     activation = (hidden * gate).astype(BF16)
     slope = gate * (1.0 + hidden * (1.0 - gate))
-    turned[...] = columns[...].reshape((rows + 2) * cells, 3 * channels).T
     term = dot(activation, cot_flat, ((0,), (0,)))
     store_rows(grads, 9 * channels, term)
     store_rows(grads_half, 9 * channels, term)
@@ -555,13 +560,17 @@
 
     wait_all(grad_copies)
     shift_cells(padded_grad, wide, grad_columns, rows, cells, (2, 1, 0))
-    input_grad = cot_flat.astype(F32)
-    for p in range(3):
+    def input_part(p):
         back = grad_columns[2 - p : 2 - p + rows].reshape(rows * cells, 3 * channels)
         taps = jnp.concatenate([conv[3 * p + q] for q in range(3)], axis=1)
-        input_grad = input_grad + dot(back, taps, ((1,), (1,)))
-    input_out[...] = input_grad.astype(BF16).reshape(input_out.shape)
-
+        before = input_sum[...] if p else cot_flat.astype(F32)
+        total = before + dot(back, taps, ((1,), (1,)))
+        if p < 2:
+            input_sum[...] = total
+        else:
+            input_out[...] = total.astype(BF16).reshape(input_out.shape)
+
+    input_part(0)
     lon_copies, out_copies = [], []
 
     def gather_chunk(n):
@@ -616,6 +625,10 @@
             )
         else:
             gather_chunk(n - 1)
+        if n < 2:
+            input_part(n + 1)
+    for p in range(len(chunks) + 1, 3):
+        input_part(p)
     wait_all(flux_lon_copies)
     total = flux_lon[0]
     for n in range(1, lon_tiles):
@@ -728,6 +741,7 @@
         pltpu.VMEM((lon_tiles, sub, channels), BF16),
         pltpu.VMEM((lon_tiles, sub, channels), BF16),
         pltpu.VMEM((members, sub, channels), BF16),
+        pltpu.VMEM((rows * cells, channels), F32),
         pltpu.VMEM((lat_tiles, small, channels), F32),
         pltpu.VMEM((members, small, channels), F32),
         pltpu.VMEM((lon_tiles, small, channels), F32),

time: 36.9 us -> 37 us (level)
  no operation moved by 1% of the time
where the time goes in v5:
time: 37 us; the launch traced here: 36.8 us
  Pallas kernels  35.6 us (96%)
  between operations  1.29 us (3%)
    pallas_call x1, Pallas kernels, fused_body(): pl.pallas_call(functools.partial(fused_kernel, (members, lat_tiles, lon_t...  33.7 us
    pallas_call x1, Pallas kernels, place(): pl.pallas_call(place_kernel, out_shape=(jax.ShapeDtypeStruct(input_grad.s...  1.88 us

profile of v5, /device:TPU:0, one launch (start us, length us, event | category | flops | bytes accessed | tf_op | source)
XLA Modules:
  0.0 36.8 jit_solution(12575532990924901034)
XLA Ops:
  1.3 33.7 %shard_map.121 = (bf16[1,4,128,256]{3,2,1,0:T(8,128)(2,1)}, bf16[4,80,256]{2,1,0:T(8,128)(2,1)}, f32[4,256]{1,0:T(4,128)}) custom-call(bf16[4,128,256]{2,1,0:T(8,128)(2,1)} %bitcast.5, bf16[4,128,256]{2,1,0:T(8,128)(2,1)} %bitcast.6, bf16[256,128]{1,0:T(8,128)(2,1)} %bitcast.7, bf16[9,256,256]{2,1,0:T(8,128)(2,1)} %conv_in.1, bf16[256,256]{1,0:T(8,128)(2,1)} %mix_in.1, ...), custom_call_target="tpu_custom_call" | custom-call | flops 1946157056 | bytes 3145728 | tf_op jit(solution)/shard_map/pallas_call | solution.py:763
  35.0 1.9 %shard_map.122 = (bf16[1,4,128,256]{3,2,1,0:T(8,128)(2,1)}, f32[320,256]{1,0:T(8,128)}, f32[4,256]{1,0:T(4,128)}) custom-call(bf16[1,4,128,256]{3,2,1,0:T(8,128)(2,1)} %get-tuple-element.6.input_grad, bf16[4,80,256]{2,1,0:T(8,128)(2,1)} %get-tuple-element.7.weight_rows, f32[4,256]{1,0:T(4,128)} %get-tuple-element.8.flux_grad), custom_call_target="tpu_custom_call" | custom-call | tf_op jit(solution)/shard_map/pallas_call | solution.py:666

commit v6 on v5

--- a/solution.py
+++ b/solution.py
@@ -253,16 +253,28 @@
         copy.wait_recv()
 
 
-def shift_cells(padded, wide, columns, rows, cells, order):
+def shift_cells(padded, wide, columns, rows, cells, order, edges=True):
     channels = padded.shape[2]
+    middle = slice(EDGE, EDGE + cells)
     for row in range(rows + 2):
-        wide[row] = padded[row].astype(F32)
+        if edges:
+            wide[row] = padded[row].astype(F32)
+        else:
+            wide[row, 0:EDGE] = jnp.zeros((EDGE, channels), F32)
+            wide[row, middle] = padded[row, middle].astype(F32)
+            wide[row, EDGE + cells :] = jnp.zeros((EDGE, channels), F32)
         for n, col in enumerate(order):
             here = slice(n * channels, (n + 1) * channels)
             if col == 1:
-                columns[row, :, here] = padded[row, EDGE : EDGE + cells]
+                columns[row, :, here] = padded[row, middle]
             else:
                 columns[row, :, here] = wide[row, pl.ds(EDGE - 1 + col, cells), :].astype(BF16)
+
+
+def turn(columns, turned, q):
+    channels = columns.shape[2] // 3
+    here = slice(q * channels, (q + 1) * channels)
+    turned[here, :] = columns[:, :, here].reshape(-1, channels).T
 
 
 def store_rows(target, first, value):
@@ -321,6 +333,9 @@
     recv_lon,
     rows_all,
     input_sum,
+    hidden_sum,
+    edge,
+    edge_part,
     flux_lat,
     flux_ens,
     flux_lon,
@@ -379,10 +394,6 @@
     padded[pl.ds(outside, 1)] = jnp.zeros((1,) + padded.shape[1:], BF16)
     padded_grad[pl.ds(outside, 1)] = jnp.zeros((1,) + padded.shape[1:], BF16)
 
-    pl.semaphore_wait(barrier, tiles - 1 + members - 1)
-    state_copies = start_all(
-        halo_copies(state_in, (0, 0), padded, rows, cells, lat, lon, lon_tiles, state_sems)
-    )
 
     loads[0].wait()
     loads[1].wait()
@@ -419,6 +430,11 @@
     flux_send[...] = share.reshape(flux_send.shape)
     flux_recv[pl.ds(flat, 1)] = flux_send[pl.ds(flat, 1)]
 
+    pl.semaphore_wait(barrier, tiles - 1 + members - 1)
+    state_copies = start_all(
+        halo_copies(state_in, (0, 0), padded, rows, cells, lat, lon, lon_tiles, state_sems)
+    )
+
     flux_copies = []
     for step in range(1, tiles):
         peer = lax.rem(flat + step, tiles)
@@ -440,19 +456,42 @@
         flux_rows[n * fields : (n + 1) * fields, :] = flux_weight[...].astype(F32)
     cot_flat = cot[...].reshape(rows * cells, channels)
     act_grad = dot(cot_flat, mix[...], ((1,), (1,)))
-    wait_all(state_copies)
-    shift_cells(padded, wide, columns, rows, cells, (0, 1, 2))
+    state_copies[0].wait_recv()
+    shift_cells(padded, wide, columns, rows, cells, (0, 1, 2), False)
     hidden = jnp.zeros((rows * cells, channels), F32)
     for p in range(3):
         hidden = hidden + dot(
             columns[p : p + rows].reshape(rows * cells, 3 * channels),
             conv[3 * p : 3 * p + 3].reshape(3 * channels, channels),
         )
-        first, last = p * (rows + 2) // 3, (p + 1) * (rows + 2) // 3
-        if last > first:
-            turned[:, first * cells : last * cells] = (
-                columns[first:last].reshape((last - first) * cells, 3 * channels).T
-            )
+    hidden_sum[...] = hidden
+    turn(columns, turned, 1)
+
+    wait_all(state_copies[1:])
+    edge[...] = jnp.zeros(edge.shape, F32)
+    cell_iota = lax.broadcasted_iota(jnp.int32, (EDGE, channels), 0)
+    for row in range(rows + 2):
+        west = padded[row, 0:EDGE].astype(F32)[EDGE - 1 :]
+        east = padded[row, EDGE + cells :].astype(F32)[:1]
+        edge[0, row : row + 1] = west
+        edge[1, row : row + 1] = east
+        kept = columns[row, 0:EDGE, 0:channels].astype(F32)
+        columns[row, 0:EDGE, 0:channels] = jnp.where(cell_iota == 0, west, kept).astype(BF16)
+        kept = columns[row, cells - EDGE :, 2 * channels :].astype(F32)
+        columns[row, cells - EDGE :, 2 * channels :] = jnp.where(cell_iota == EDGE - 1, east, kept).astype(BF16)
+    for side in range(2):
+        cells_there = edge[side].astype(BF16)
+        for p in range(3):
+            edge_part[side, p] = dot(cells_there, conv[3 * p + 2 * side])
+        for row in range(rows):
+            at = row * cells + side * (cells - 1)
+            added = hidden_sum[at : at + 1]
+            for p in range(3):
+                added = added + edge_part[side, p, row + p : row + p + 1]
+            hidden_sum[at : at + 1] = added
+    hidden = hidden_sum[...]
+    turn(columns, turned, 0)
+    turn(columns, turned, 2)
     gate = jax.nn.sigmoid(hidden)
     activation = (hidden * gate).astype(BF16)
     slope = gate * (1.0 + hidden * (1.0 - gate))
@@ -702,6 +741,7 @@
     halo = (rows + 2, cells + 2 * EDGE, channels)
     spread = (rows + 2, cells, 3 * channels)
     small = 2 * fields
+    edge_rows = -(-(rows + 2) // EDGE) * EDGE
     size = 2 * EDGE
     chunks = [(at, min(size, sub - at)) for at in range(0, sub, size)]
 
@@ -742,6 +782,9 @@
         pltpu.VMEM((lon_tiles, sub, channels), BF16),
         pltpu.VMEM((members, sub, channels), BF16),
         pltpu.VMEM((rows * cells, channels), F32),
+        pltpu.VMEM((rows * cells, channels), F32),
+        pltpu.VMEM((2, edge_rows, channels), F32),
+        pltpu.VMEM((2, 3, edge_rows, channels), F32),
         pltpu.VMEM((lat_tiles, small, channels), F32),
         pltpu.VMEM((members, small, channels), F32),
         pltpu.VMEM((lon_tiles, small, channels), F32),

time: 37 us -> 36.4 us (0.984)
  Pallas kernels: 35.6 us -> 34.9 us
    pallas_call x1, Pallas kernels: 33.7 us -> 33 us  [fused_body(): pl.pallas_call(functools.partial(fused_kernel, (members, lat_tiles, lon_t...]
where the time goes in v6:
time: 36.4 us; the launch traced here: 36.2 us
  Pallas kernels  34.9 us (96%)
  between operations  1.29 us (4%)
    pallas_call x1, Pallas kernels, fused_body(): pl.pallas_call(functools.partial(fused_kernel, (members, lat_tiles, lon_t...  33 us
    pallas_call x1, Pallas kernels, place(): pl.pallas_call(place_kernel, out_shape=(jax.ShapeDtypeStruct(input_grad.s...  1.88 us

profile of v6, /device:TPU:0, one launch (start us, length us, event | category | flops | bytes accessed | tf_op | source)
XLA Modules:
  0.0 36.2 jit_solution(8764462731967950884)
XLA Ops:
  1.3 33.0 %shard_map.121 = (bf16[1,4,128,256]{3,2,1,0:T(8,128)(2,1)}, bf16[4,80,256]{2,1,0:T(8,128)(2,1)}, f32[4,256]{1,0:T(4,128)}) custom-call(bf16[4,128,256]{2,1,0:T(8,128)(2,1)} %bitcast.5, bf16[4,128,256]{2,1,0:T(8,128)(2,1)} %bitcast.6, bf16[256,128]{1,0:T(8,128)(2,1)} %bitcast.7, bf16[9,256,256]{2,1,0:T(8,128)(2,1)} %conv_in.1, bf16[256,256]{1,0:T(8,128)(2,1)} %mix_in.1, ...), custom_call_target="tpu_custom_call" | custom-call | flops 1946157056 | bytes 3145728 | tf_op jit(solution)/shard_map/pallas_call | solution.py:806
  34.3 1.9 %shard_map.122 = (bf16[1,4,128,256]{3,2,1,0:T(8,128)(2,1)}, f32[320,256]{1,0:T(8,128)}, f32[4,256]{1,0:T(4,128)}) custom-call(bf16[1,4,128,256]{3,2,1,0:T(8,128)(2,1)} %get-tuple-element.6.input_grad, bf16[4,80,256]{2,1,0:T(8,128)(2,1)} %get-tuple-element.7.weight_rows, f32[4,256]{1,0:T(4,128)} %get-tuple-element.8.flux_grad), custom_call_target="tpu_custom_call" | custom-call | tf_op jit(solution)/shard_map/pallas_call | solution.py:705

commit v7 on v6

--- a/solution.py
+++ b/solution.py
@@ -328,6 +328,8 @@
     grads_half,
     recv_lat,
     sum_lat,
+    recv_pair,
+    sum_pair,
     recv_ens,
     sum_ens,
     recv_lon,
@@ -568,26 +570,34 @@
         def _():
             tap_grads(grads, part * taps, min((part + 1) * taps, 9))
 
-    ens_copies = []
+    high, low = ens // 2, lax.rem(ens, 2)
+    partners = (high * 2 + 1 - low, (1 - high) * 2 + low)
+    halves = [pl.ds(0, lon_tiles // 2), pl.ds(lon_tiles // 2, lon_tiles // 2)]
+
+    def pair_copies(n, phase):
+        here = pl.ds(chunks[n][0], chunks[n][1])
+        copies = []
+        for half, span in enumerate(halves):
+            if phase == 0:
+                away = (slice(None), 1 - low) if half == 0 else (1 - high, slice(None))
+                source = sum_lat.at[span, away[0], away[1], here]
+                target = recv_pair.at[span, :, here]
+                partner = partners[half]
+            else:
+                source = sum_pair.at[span, 1 - high if half == 0 else 1 - low, here]
+                target = recv_ens.at[span, here]
+                partner = partners[1 - half]
+            sem = n * 4 + phase * 2 + half
+            copies.append(remote(source, target, ens_sems[0].at[sem], ens_sems[1].at[sem], {"ens": partner}))
+        return copies
+
+    first_copies, second_copies = [], []
     for n, (at, count) in enumerate(chunks):
         wait_all(lat_copies[n])
         own = grads[pl.ds(lat, 1), :, at : at + count]
         part = (own[0] + recv_lat[:, at : at + count].astype(F32)).astype(BF16)
-        sum_lat[:, :, at : at + count] = part.reshape(lon_tiles, members, count, channels)
-        ens_copies.append(
-            start_all(
-                exchange(
-                    "ens",
-                    members,
-                    ens,
-                    lambda to: sum_lat.at[:, to, pl.ds(at, count)],
-                    lambda me: recv_ens.at[me, :, pl.ds(at, count)],
-                    ens_sems,
-                    n * members,
-                )
-            )
-        )
-    recv_ens[pl.ds(ens, 1)] = sum_lat[:, pl.ds(ens, 1)].reshape((1,) + recv_ens.shape[1:])
+        sum_lat[:, :, :, at : at + count] = part.reshape(lon_tiles, 2, 2, count, channels)
+        first_copies.append(start_all(pair_copies(n, 0)))
     wait_all(flux_lat_copies)
     total = flux_lat[0]
     for n in range(1, lat_tiles):
@@ -633,27 +643,47 @@
             )
         )
 
-    for n, (at, count) in enumerate(chunks):
-        wait_all(ens_copies[n])
-        total = recv_ens[0, :, at : at + count].astype(F32)
-        for other in range(1, members):
-            total = total + recv_ens[other, :, at : at + count].astype(F32)
-        sum_ens[:, at : at + count] = total.astype(BF16)
+    def second_chunk(n):
+        wait_all(first_copies[n])
+        here = pl.ds(chunks[n][0], chunks[n][1])
+        for half, span in enumerate(halves):
+            if half == 0:
+                own = sum_lat[span, :, pl.ds(low, 1), here]
+            else:
+                own = sum_lat[span, pl.ds(high, 1), :, here]
+            came = recv_pair[span, :, here].astype(F32)
+            sum_pair[span, :, here] = (own.reshape(came.shape).astype(F32) + came).astype(BF16)
+        second_copies.append(start_all(pair_copies(n, 1)))
+
+    def lon_chunk(n):
+        at, count = chunks[n]
+        here = pl.ds(at, count)
+        wait_all(second_copies[n])
+        for half, span in enumerate(halves):
+            own = sum_pair[span, pl.ds(high if half == 0 else low, 1), here]
+            came = recv_ens[span, here].astype(F32)
+            sum_ens[span, here] = (own.reshape(came.shape).astype(F32) + came).astype(BF16)
         lon_copies.append(
             start_all(
                 exchange(
                     "ox",
                     lon_tiles,
                     lon,
-                    lambda to: sum_ens.at[to, pl.ds(at, count)],
-                    lambda me: recv_lon.at[me, pl.ds(at, count)],
+                    lambda to: sum_ens.at[to, here],
+                    lambda me: recv_lon.at[me, here],
                     lon_sems,
                     n * lon_tiles,
                 )
             )
         )
-        recv_lon[pl.ds(lon, 1), at : at + count] = sum_ens[pl.ds(lon, 1), at : at + count]
-        if n == 0:
+        recv_lon[pl.ds(lon, 1), here] = sum_ens[pl.ds(lon, 1), here]
+
+    for n in range(len(chunks) + 2):
+        if n < len(chunks):
+            second_chunk(n)
+        if 0 <= n - 1 < len(chunks):
+            lon_chunk(n - 1)
+        if n == 1:
             wait_all(flux_ens_copies)
             total = flux_ens[0]
             for other in range(1, members):
@@ -662,12 +692,10 @@
             flux_lon_copies = start_all(
                 exchange("ox", lon_tiles, lon, lambda to: flux_lon.at[lon], lambda me: flux_lon.at[me], flux_lon_sems)
             )
-        else:
-            gather_chunk(n - 1)
+        if 0 <= n - 2 < len(chunks) - 1:
+            gather_chunk(n - 2)
         if n < 2:
             input_part(n + 1)
-    for p in range(len(chunks) + 1, 3):
-        input_part(p)
     wait_all(flux_lon_copies)
     total = flux_lon[0]
     for n in range(1, lon_tiles):
@@ -678,7 +706,7 @@
         wait_all(copies)
     weight_out[...] = rows_all[...]
     started = state_copies + flux_copies + grad_copies + flux_lat_copies + flux_ens_copies + flux_lon_copies
-    for copies in [started] + lat_copies + ens_copies + lon_copies + out_copies:
+    for copies in [started] + lat_copies + first_copies + second_copies + lon_copies + out_copies:
         for copy in copies:
             copy.wait_send()
 
@@ -776,8 +804,10 @@
         pltpu.VMEM((lat_tiles, pieces, sub, channels), F32),
         pltpu.VMEM((lat_tiles, pieces, sub, channels), BF16),
         pltpu.VMEM((pieces, sub, channels), BF16),
-        pltpu.VMEM((lon_tiles, members, sub, channels), BF16),
-        pltpu.VMEM((members, lon_tiles, sub, channels), BF16),
+        pltpu.VMEM((lon_tiles, 2, 2, sub, channels), BF16),
+        pltpu.VMEM((lon_tiles, 2, sub, channels), BF16),
+        pltpu.VMEM((lon_tiles, 2, sub, channels), BF16),
+        pltpu.VMEM((lon_tiles, sub, channels), BF16),
         pltpu.VMEM((lon_tiles, sub, channels), BF16),
         pltpu.VMEM((lon_tiles, sub, channels), BF16),
         pltpu.VMEM((members, sub, channels), BF16),
@@ -837,7 +867,7 @@
     grad_rows = (conv_weight.shape[0] + 1) * state.shape[3]
     whole_tiles = grad_rows % (lat_tiles * lon_tiles * members * EDGE) == 0
     whole_taps = grad_rows // lat_tiles % state.shape[3] == 0
-    fused = lat_tiles == 2 and lon_tiles > 1 and whole_tiles and whole_taps
+    fused = lat_tiles == 2 and members == 4 and lon_tiles % 2 == 0 and whole_tiles and whole_taps
     return (fused_body if fused else body)(state, state_cot, flux_cot, conv_weight, *rest)
 
 

time: 36.4 us -> 37.1 us (1.019)
  Pallas kernels: 34.9 us -> 35.6 us
    pallas_call x1, Pallas kernels: 33 us -> 33.7 us  [fused_body(): pl.pallas_call(functools.partial(fused_kernel, (members, lat_tiles, lon_t...]
where the time goes in v7:
time: 37.1 us; the launch traced here: 36.9 us
  Pallas kernels  35.6 us (96%)
  between operations  1.29 us (3%)
    pallas_call x1, Pallas kernels, fused_body(): pl.pallas_call(functools.partial(fused_kernel, (members, lat_tiles, lon_t...  33.7 us
    pallas_call x1, Pallas kernels, place(): pl.pallas_call(place_kernel, out_shape=(jax.ShapeDtypeStruct(input_grad.s...  1.88 us

profile of v7, /device:TPU:0, one launch (start us, length us, event | category | flops | bytes accessed | tf_op | source)
XLA Modules:
  0.0 36.9 jit_solution(11096659091144981941)
XLA Ops:
  1.3 33.7 %shard_map.121 = (bf16[1,4,128,256]{3,2,1,0:T(8,128)(2,1)}, bf16[4,80,256]{2,1,0:T(8,128)(2,1)}, f32[4,256]{1,0:T(4,128)}) custom-call(bf16[4,128,256]{2,1,0:T(8,128)(2,1)} %bitcast.5, bf16[4,128,256]{2,1,0:T(8,128)(2,1)} %bitcast.6, bf16[256,128]{1,0:T(8,128)(2,1)} %bitcast.7, bf16[9,256,256]{2,1,0:T(8,128)(2,1)} %conv_in.1, bf16[256,256]{1,0:T(8,128)(2,1)} %mix_in.1, ...), custom_call_target="tpu_custom_call" | custom-call | flops 1946157056 | bytes 3145728 | tf_op jit(solution)/shard_map/pallas_call | solution.py:836
  35.0 1.9 %shard_map.122 = (bf16[1,4,128,256]{3,2,1,0:T(8,128)(2,1)}, f32[320,256]{1,0:T(8,128)}, f32[4,256]{1,0:T(4,128)}) custom-call(bf16[1,4,128,256]{3,2,1,0:T(8,128)(2,1)} %get-tuple-element.6.input_grad, bf16[4,80,256]{2,1,0:T(8,128)(2,1)} %get-tuple-element.7.weight_rows, f32[4,256]{1,0:T(4,128)} %get-tuple-element.8.flux_grad), custom_call_target="tpu_custom_call" | custom-call | tf_op jit(solution)/shard_map/pallas_call | solution.py:733

commit v8 on v6

--- a/solution.py
+++ b/solution.py
@@ -742,7 +742,7 @@
     spread = (rows + 2, cells, 3 * channels)
     small = 2 * fields
     edge_rows = -(-(rows + 2) // EDGE) * EDGE
-    size = 2 * EDGE
+    size = 3 * EDGE
     chunks = [(at, min(size, sub - at)) for at in range(0, sub, size)]
 
     def pair(count):

time: 36.4 us -> 36 us (0.989)
  Pallas kernels: 34.9 us -> 34.5 us
    pallas_call x1, Pallas kernels: 33 us -> 32.6 us  [fused_body(): pl.pallas_call(functools.partial(fused_kernel, (members, lat_tiles, lon_t...]
where the time goes in v8:
time: 36 us; the launch traced here: 35.7 us
  Pallas kernels  34.5 us (96%)
  between operations  1.29 us (4%)
    pallas_call x1, Pallas kernels, fused_body(): pl.pallas_call(functools.partial(fused_kernel, (members, lat_tiles, lon_t...  32.6 us
    pallas_call x1, Pallas kernels, place(): pl.pallas_call(place_kernel, out_shape=(jax.ShapeDtypeStruct(input_grad.s...  1.88 us

profile of v8, /device:TPU:0, one launch (start us, length us, event | category | flops | bytes accessed | tf_op | source)
XLA Modules:
  0.0 35.7 jit_solution(5227959392286747332)
XLA Ops:
  1.3 32.6 %shard_map.121 = (bf16[1,4,128,256]{3,2,1,0:T(8,128)(2,1)}, bf16[4,80,256]{2,1,0:T(8,128)(2,1)}, f32[4,256]{1,0:T(4,128)}) custom-call(bf16[4,128,256]{2,1,0:T(8,128)(2,1)} %bitcast.5, bf16[4,128,256]{2,1,0:T(8,128)(2,1)} %bitcast.6, bf16[256,128]{1,0:T(8,128)(2,1)} %bitcast.7, bf16[9,256,256]{2,1,0:T(8,128)(2,1)} %conv_in.1, bf16[256,256]{1,0:T(8,128)(2,1)} %mix_in.1, ...), custom_call_target="tpu_custom_call" | custom-call | flops 1946157056 | bytes 3145728 | tf_op jit(solution)/shard_map/pallas_call | solution.py:806
  33.9 1.9 %shard_map.122 = (bf16[1,4,128,256]{3,2,1,0:T(8,128)(2,1)}, f32[320,256]{1,0:T(8,128)}, f32[4,256]{1,0:T(4,128)}) custom-call(bf16[1,4,128,256]{3,2,1,0:T(8,128)(2,1)} %get-tuple-element.6.input_grad, bf16[4,80,256]{2,1,0:T(8,128)(2,1)} %get-tuple-element.7.weight_rows, f32[4,256]{1,0:T(4,128)} %get-tuple-element.8.flux_grad), custom_call_target="tpu_custom_call" | custom-call | tf_op jit(solution)/shard_map/pallas_call | solution.py:705

commit v9 on v8

--- a/solution.py
+++ b/solution.py
@@ -742,8 +742,7 @@
     spread = (rows + 2, cells, 3 * channels)
     small = 2 * fields
     edge_rows = -(-(rows + 2) // EDGE) * EDGE
-    size = 3 * EDGE
-    chunks = [(at, min(size, sub - at)) for at in range(0, sub, size)]
+    chunks = [(0, sub)]
 
     def pair(count):
         return (pltpu.SemaphoreType.DMA((count,)), pltpu.SemaphoreType.DMA((count,)))

time: 36 us -> 38 us (1.056)
  Pallas kernels: 34.5 us -> 36.5 us
    pallas_call x1, Pallas kernels: 32.6 us -> 34.6 us  [fused_body(): pl.pallas_call(functools.partial(fused_kernel, (members, lat_tiles, lon_t...]
where the time goes in v9:
time: 38 us; the launch traced here: 37.8 us
  Pallas kernels  36.5 us (96%)
  between operations  1.29 us (3%)
    pallas_call x1, Pallas kernels, fused_body(): pl.pallas_call(functools.partial(fused_kernel, (members, lat_tiles, lon_t...  34.6 us
    pallas_call x1, Pallas kernels, place(): pl.pallas_call(place_kernel, out_shape=(jax.ShapeDtypeStruct(input_grad.s...  1.88 us

profile of v9, /device:TPU:0, one launch (start us, length us, event | category | flops | bytes accessed | tf_op | source)
XLA Modules:
  0.0 37.8 jit_solution(8408801630821486748)
XLA Ops:
  1.3 34.6 %shard_map.121 = (bf16[1,4,128,256]{3,2,1,0:T(8,128)(2,1)}, bf16[4,80,256]{2,1,0:T(8,128)(2,1)}, f32[4,256]{1,0:T(4,128)}) custom-call(bf16[4,128,256]{2,1,0:T(8,128)(2,1)} %bitcast.5, bf16[4,128,256]{2,1,0:T(8,128)(2,1)} %bitcast.6, bf16[256,128]{1,0:T(8,128)(2,1)} %bitcast.7, bf16[9,256,256]{2,1,0:T(8,128)(2,1)} %conv_in.1, bf16[256,256]{1,0:T(8,128)(2,1)} %mix_in.1, ...), custom_call_target="tpu_custom_call" | custom-call | flops 1946157056 | bytes 3145728 | tf_op jit(solution)/shard_map/pallas_call | solution.py:805
  35.9 1.9 %shard_map.122 = (bf16[1,4,128,256]{3,2,1,0:T(8,128)(2,1)}, f32[320,256]{1,0:T(8,128)}, f32[4,256]{1,0:T(4,128)}) custom-call(bf16[1,4,128,256]{3,2,1,0:T(8,128)(2,1)} %get-tuple-element.6.input_grad, bf16[4,80,256]{2,1,0:T(8,128)(2,1)} %get-tuple-element.7.weight_rows, f32[4,256]{1,0:T(4,128)} %get-tuple-element.8.flux_grad), custom_call_target="tpu_custom_call" | custom-call | tf_op jit(solution)/shard_map/pallas_call | solution.py:705
